TPU v7x, 512 devices: a whole 4x8x8 slice. The times are simulated.
512 devices in a mesh: dp: 64 (over z_hi, y, core), pre: 8 (over x, z_lo).
Axes of the slice: x: 4, y: 8, z: 8 (z_hi: 4, z_lo: 2; z = z_hi * 2 + z_lo), core: 2. Of those that a mesh axis runs over, the one named last changes fastest.
Arguments:
- inputs: bfloat16 [8192, 4096], P('dp'), may hold values from -12 to 12, as said below
- weight: bfloat16 [4096, 1024], P(None, 'pre'), may hold values from -0.09375 to 0.09375
- cotangent: bfloat16 [8192, 1024], P('dp', 'pre'), may hold values from -12 to 12, as said below
Outputs:
- outputs: bfloat16 [8192, 1024], P('dp', 'pre')
- update: bfloat16 [8, 512, 1024], P(None, 'pre')
Inputs may be any that keep to these rules, and one draw needn't show every extreme that they name: `inputs`: activations with unequal scales across features. `cotangent`: gradients with unequal scales across features.
All inputs are finite; a program needn't handle non-finite values.
Results may differ from a plain program's by a relative error of at most 0.0079.
Values may be sent and summed in bfloat16 or wider, within the bound.
A program may use at most 64 MiB of HBM per device.

v0:
```python
import math

import jax
import jax.numpy as jnp
from jax import lax
from jax.sharding import PartitionSpec as P

D = 4096
BLOCK = 512
CB = 2
ITERS = 3


DAMPING = 0.1
HIGH = lax.Precision.HIGHEST


def batch_dot(former, latter):
    return jnp.einsum(
        "sij,sjk->sik", former, latter, precision=HIGH, preferred_element_type=jnp.float32
    )


def on_device(inputs, weight, cotangent):
    groups = lax.axis_size("dp")
    members = lax.axis_size("pre")
    group_id = lax.axis_index("dp")
    member_id = lax.axis_index("pre")
    slab_rows = BLOCK // members
    blocks_all = D // BLOCK * CB
    rounds = max(1, blocks_all // groups)
    sharers = max(1, groups // blocks_all)
    col_width = BLOCK // sharers
    copy_id = group_id // blocks_all
    outputs = jnp.dot(inputs, weight, preferred_element_type=jnp.float32).astype(jnp.bfloat16)
    partial_value = lax.dot_general(
        inputs, cotangent, (((0,), (0,)), ((), ())), preferred_element_type=jnp.float32
    )
    owned_ids = (group_id + groups * jnp.arange(rounds, dtype=jnp.int32)) % blocks_all
    row_offsets = owned_ids // CB * BLOCK
    col_offsets = owned_ids % CB * BLOCK
    gradient = lax.psum(partial_value, "dp")
    row_bands = jax.vmap(lambda offset: lax.dynamic_slice_in_dim(gradient, offset, BLOCK, 0))(
        row_offsets
    )
    wide_band = lax.all_gather(row_bands, "pre", axis=2, tiled=True)
    tile_grad = jax.vmap(
        lambda row_band, offset: lax.dynamic_slice_in_dim(row_band, offset, BLOCK, 1)
    )(wide_band, col_offsets)
    first_row = member_id * slab_rows
    own_rows = lax.dynamic_slice_in_dim(tile_grad, first_row, slab_rows, 1)
    own_cols = lax.dynamic_slice_in_dim(tile_grad, first_row, slab_rows, 2)
    left_rows = jnp.einsum(
        "sij,skj->sik", own_rows, tile_grad, precision=HIGH, preferred_element_type=jnp.float32
    )
    right_rows = jnp.einsum(
        "sji,sjk->sik", own_cols, tile_grad, precision=HIGH, preferred_element_type=jnp.float32
    )
    stat_rows = jnp.stack([left_rows, right_rows], axis=1).reshape(rounds * 2, slab_rows, BLOCK)
    tile_energy = jnp.sum(tile_grad * tile_grad, axis=(1, 2))
    energy = jnp.stack([tile_energy, tile_energy], axis=1).reshape(rounds * 2)
    unit_rows = (jnp.arange(BLOCK)[None, :] == (first_row + jnp.arange(slab_rows))[:, None]).astype(
        jnp.float32
    )
    unit_eye = jnp.eye(BLOCK, dtype=jnp.float32)
    state_rows = stat_rows + (DAMPING * energy / BLOCK)[:, None, None] * unit_rows[None]
    root_rows = unit_rows[None]
    for iteration in range(ITERS):
        full_state = lax.all_gather(state_rows, "pre", axis=1, tiled=True)
        if iteration == 0:
            frob_norm = jnp.sqrt(jnp.sum(full_state * full_state, axis=(1, 2)))
            full_state = full_state / frob_norm[:, None, None]
            state_rows = state_rows / frob_norm[:, None, None]
            root_rows = unit_rows[None] * (frob_norm ** (-0.25))[:, None, None]
        factor = (5.0 * unit_eye - full_state) * 0.25
        square = batch_dot(factor, factor)
        square_rows = lax.dynamic_slice_in_dim(square, first_row, slab_rows, 1)
        fourth_rows = batch_dot(square_rows, square)
        state_rows = batch_dot(fourth_rows, full_state)
        root_rows = batch_dot(root_rows, factor)
    root_half = root_rows.astype(jnp.bfloat16).reshape(rounds, 2, slab_rows, BLOCK)
    right_full = lax.all_gather(root_half[:, 1], "pre", axis=1, tiled=True)
    right_cols = lax.dynamic_slice_in_dim(right_full, copy_id * col_width, col_width, 2)
    tile_half = tile_grad.astype(jnp.bfloat16)
    half_prod = jnp.einsum(
        "sij,sjk->sik", root_half[:, 0], tile_half, preferred_element_type=jnp.float32
    ).astype(jnp.bfloat16)
    piece_rows = jnp.einsum(
        "sij,sjk->sik", half_prod, right_cols, preferred_element_type=jnp.float32
    )
    piece_rows = (piece_rows * math.sqrt(BLOCK)).astype(jnp.bfloat16)
    collected = lax.all_gather(piece_rows[None], "dp", axis=0, tiled=True)
    ordered = (
        collected[:, 0]
        .reshape(sharers, blocks_all, slab_rows, col_width)
        .transpose(1, 2, 0, 3)
        .reshape(blocks_all, slab_rows, BLOCK)
    )
    update = (
        ordered.reshape(D // BLOCK, CB, slab_rows, BLOCK)
        .transpose(0, 2, 1, 3)
        .reshape(D // BLOCK, slab_rows, CB * BLOCK)
    )
    return (outputs, update)


def solution(mesh):
    placed = (P("dp", None), P(None, "pre"), P("dp", "pre"))
    return jax.shard_map(
        on_device,
        mesh=mesh,
        in_specs=placed,
        out_specs=(P("dp", "pre"), P(None, "pre", None)),
        check_vma=False,
    )
```

profile of v0, /device:TPU:1, one launch (start us, length us, event | category | flops | bytes accessed | tf_op | source)
XLA Modules:
  0.0 959.6 jit_solution(18308971646947978580)
XLA Ops:
  7.2 0.0 copy-start
  7.2 0.0 all-reduce.2.cloned.1.call-start
  7.2 1.2 copy-done
  8.4 2.6 fusion.56
  11.0 0.0 all-reduce.2.cloned.1.call-update
  11.0 0.0 all-gather.15.cloned.1.call-start
  11.1 566.4 %all-reduce.2.cloned.1.call-done = f32[4096,128]{1,0:T(8,128)} async-done(((f32[4096,128]{1,0:T(8,128)}), f32[4096,128]{1,0:T(8,128)}) %all-reduce.2.cloned.1.call-update) | async-done | bytes 2097168 | tf_op jit(solution)/shard_map/psum | solution.py:42
  577.4 1.7 constant_dynamic-slice_fusion
  579.1 0.0 all-gather.15.cloned.1.call-update
  579.1 0.0 all-gather.9.cloned.1.call-start
  579.2 0.1 fusion.41
  579.3 53.0 %all-gather.15.cloned.1.call-done = f32[512,1024]{1,0:T(8,128)} async-done(((f32[512,128]{1,0:T(8,128)}), f32[512,1024]{1,0:T(8,128)}) %all-gather.15.cloned.1.call-update) | async-done | bytes 2097168 | tf_op jit(solution)/shard_map/all_gather | solution.py:46
  632.3 0.0 copy-start.4
  632.4 2.2 multiply_reduce_fusion.1
  634.6 0.7 fusion.48
  635.3 2.4 convolution_bitcast_fusion.1
  637.8 0.0 copy-done.4
  637.8 0.8 convolution_bitcast_fusion
  638.5 0.8 fusion.29
  639.3 0.0 all-gather.9.cloned.1.call-update
  639.3 0.0 all-gather.11.cloned.1.call-start
  639.4 0.1 fusion.26
  639.5 0.0 copy-start.2
  639.5 58.7 %all-gather.9.cloned.1.call-done = f32[2,512,512]{2,1,0:T(8,128)} async-done(((f32[2,64,512]{2,1,0:T(8,128)}), f32[2,512,512]{2,1,0:T(8,128)}) %all-gather.9.cloned.1.call-update) | async-done | bytes 2097168 | tf_op jit(solution)/shard_map/all_gather | solution.py:69
  698.3 0.0 copy-start.5
  698.3 2.1 multiply_reduce_fusion
  700.4 0.1 copy-done.5
  700.5 4.0 fusion.3
  704.5 1.4 fusion.33
  705.9 2.2 fusion.54
  708.1 0.0 all-gather.11.cloned.1.call-update
  708.1 0.2 all-gather.13.cloned.1.call-start
  708.3 56.7 %all-gather.11.cloned.1.call-done = f32[2,512,512]{2,1,0:T(8,128)} async-done(((f32[2,64,512]{2,1,0:T(8,128)}), f32[2,512,512]{2,1,0:T(8,128)}) %all-gather.11.cloned.1.call-update) | async-done | bytes 2097168 | tf_op jit(solution)/shard_map/all_gather | solution.py:69
  765.0 0.0 copy-done.2
  765.0 6.0 fusion.5
  771.0 0.0 copy-start.1
  771.0 1.4 fusion.31
  772.4 0.2 copy-done.1
  772.6 2.1 fusion.57
  774.7 0.0 all-gather.13.cloned.1.call-update
  774.7 0.0 all-gather.17.cloned.1.call-start
  774.8 0.0 copy-start.3
  774.8 3.7 fusion.4
  778.5 0.0 copy-done.3
  778.5 1.5 fusion.6
  780.0 0.0 copy-start.6
  780.0 51.6 %all-gather.13.cloned.1.call-done = f32[2,512,512]{2,1,0:T(8,128)} async-done(((f32[2,64,512]{2,1,0:T(8,128)}), f32[2,512,512]{2,1,0:T(8,128)}) %all-gather.13.cloned.1.call-update) | async-done | bytes 2097168 | tf_op jit(solution)/shard_map/all_gather | solution.py:69
  831.6 3.4 fusion.10
  835.0 24.3 %all-gather.1 = bf16[1,1,512,512]{3,2,1,0:T(8,128)(2,1)S(1)} all-gather(bf16[1,1,64,512]{3,2,1,0:T(8,128)(2,1)S(1)} %slice.37), channel_id=3, replica_groups=mesh['dp'=64,'pre'=8] {'pre'}, dimensions={2}, use_global_device_ids=true | all-gather | bytes 589824 | tf_op jit(solution)/shard_map/all_gather | solution.py:82
  859.3 2.2 fusion.15
  861.5 0.0 all-gather.17.cloned.1.call-update
  861.5 0.0 copy-done.6
  861.5 1.0 convolution_convert_fusion.1
  862.6 86.5 %all-gather.17.cloned.1.call-done = bf16[4096,128]{1,0:T(8,128)(2,1)} async-done(((bf16[64,128]{1,0:T(8,128)(2,1)}), bf16[4096,128]{1,0:T(8,128)(2,1)}) %all-gather.17.cloned.1.call-update) | async-done | bytes 1048592 | tf_op jit(solution)/shard_map/all_gather | solution.py:92
  949.1 2.1 copy.10
  951.2 0.4 reshape_reshape.3
  951.6 1.1 copy.8
  (3 shorter events, 0.0 us)
Async XLA Ops:
  7.2 1.2 copy-start
  7.2 570.3 %all-reduce.2.cloned.1.call-start = ((), (), s32[]{:S(2)}) async-start(), calls=%async_computation | async-start | bytes 4194304 | tf_op jit(solution)/shard_map/psum | solution.py:42
  11.0 621.4 %all-gather.15.cloned.1.call-start = ((), (), s32[]{:S(2)}) async-start(), calls=%async_computation.4 | async-start | bytes 2359296 | tf_op jit(solution)/shard_map/all_gather | solution.py:46
  579.1 119.1 %all-gather.9.cloned.1.call-start = ((), (), s32[]{:S(2)}) async-start(), calls=%async_computation.1 | async-start | bytes 2359296 | tf_op jit(solution)/shard_map/all_gather | solution.py:69
  632.3 5.4 copy-start.4
  639.3 125.7 %all-gather.11.cloned.1.call-start = ((), (), s32[]{:S(2)}) async-start(), calls=%async_computation.2 | async-start | bytes 2359296 | tf_op jit(solution)/shard_map/all_gather | solution.py:69
  639.5 125.5 %copy-start.2 = (f32[512,512]{1,0:T(8,128)}, f32[512,512]{1,0:T(8,128)S(1)}, u32[]{:S(2)}) copy-start(f32[512,512]{1,0:T(8,128)S(1)} %fusion.26) | copy-start | bytes 3145732
  698.3 2.2 copy-start.5
  708.1 123.5 %all-gather.13.cloned.1.call-start = ((), (), s32[]{:S(2)}) async-start(), calls=%async_computation.3 | async-start | bytes 2359296 | tf_op jit(solution)/shard_map/all_gather | solution.py:69
  771.0 1.6 copy-start.1
  774.7 174.4 %all-gather.17.cloned.1.call-start = ((), (), s32[]{:S(2)}) async-start(), calls=%async_computation.5 | async-start | bytes 1064960 | tf_op jit(solution)/shard_map/all_gather | solution.py:92
  774.8 3.7 copy-start.3
  780.0 81.5 %copy-start.6 = (bf16[4096,128]{1,0:T(8,128)(2,1)S(1)}, bf16[4096,128]{1,0:T(8,128)(2,1)}, u32[]{:S(2)}) copy-start(bf16[4096,128]{1,0:T(8,128)(2,1)} %param.4) | copy-start | bytes 3145732
Sparse Core Ops, SparseCore 0:
  11.1 566.2 all-reduce.1
  580.2 52.0 all-gather.14
  639.5 58.7 all-gather.8
  708.2 56.7 all-gather.10
  774.8 56.7 all-gather.12
  861.6 87.3 all-gather.16
where the time goes:
time: 960 us
  waiting for transfers between devices  873 us (91%)
  matrix products  34.5 us (4%)
  blocking collectives  24.3 us (3%)
  between operations  14.3 us (1%)
    psum x1, waiting for transfers between devices, on_device(): gradient = lax.psum(partial_value, 'dp')  566 us
    all_gather x3, waiting for transfers between devices, on_device(): full_state = lax.all_gather(state_rows, 'pre', axis=1, tiled=True)  167 us
    all_gather x1, waiting for transfers between devices, on_device(): collected = lax.all_gather(piece_rows[None], 'dp', axis=0, tiled=True)  86.5 us
    all_gather x1, waiting for transfers between devices, on_device(): wide_band = lax.all_gather(row_bands, 'pre', axis=2, tiled=True)  53 us
    dot_general x9, matrix products, batch_dot(): jnp.einsum('sij,sjk->sik', former, latter, precision=HIGH, preferred_elem...  25.6 us
    all_gather x1, blocking collectives, on_device(): right_full = lax.all_gather(root_half[:, 1], 'pre', axis=1, tiled=True)  24.3 us
  transfers between devices with their start and end apart: 6, of which 6 were waited for; matrix products, arithmetic and copies ran while one was open for 1% of the time, Pallas kernels for 0%

commit v1 on v0

v1 whole, which is shorter than its diff:
```python
import math

import jax
import jax.numpy as jnp
from jax import lax
from jax.experimental import pallas as pl
from jax.experimental.pallas import tpu as pltpu
from jax.sharding import PartitionSpec as P

D = 4096
BLOCK = 512
CB = 2
HALF = BLOCK // 2
DAMPING = 0.1
MESH = pl.DeviceIdType.MESH
BF16 = jnp.bfloat16
F32 = jnp.float32

Y_ORDER = (4, 3, 5, 2, 6, 1, 7, 0)


def nn(a, b):
    return lax.dot_general(a, b, (((1,), (0,)), ((), ())), preferred_element_type=F32)


def nt(a, b):
    return lax.dot_general(a, b, (((1,), (1,)), ((), ())), preferred_element_type=F32)


def kernel(
    a_hbm, w_hbm, b_hbm, out_ref, upd_hbm,
    a_v, w_v, b_v, a_s, b_s, part, rs_buf, tile, u_ref,
    m0, m1, m2, t0, b0, b1, xr, hbuf, rbuf, osrc, oland,
    load_sem, as_send, as_recv, bs_send, bs_recv, rs_send, rs_recv,
    ag_send, ag_recv, th_send, th_recv, ex_send, ex_recv,
    o_send, o_recv, of_send, of_recv, fin_sem,
):
    dp = lax.axis_index("dp")
    pre = lax.axis_index("pre")
    zh, y, core = dp // 16, (dp // 2) % 8, dp % 2
    x, zl = pre // 2, pre % 2
    z = zh * 2 + zl
    c = x // 2
    x_pair = c * 2 + (1 - x % 2)
    x_mirror = 3 - x

    def dev(zh_, y_, core_, x_, zl_):
        return ((zh_ * 8 + y_) * 2 + core_, x_ * 2 + zl_)

    sibling = dev(zh, y, 1 - core, x, zl)

    def rs_peer(dy, dzh):
        return dev((zh + dzh) % 4, (y + dy) % 8, core, x, zl)

    def ag_peer(dx, dz):
        z_ = (z + dz) % 8
        return dev(z_ // 2, y, core, x_pair if dx else x, z_ % 2)

    def out_peer(dx, dy):
        return dev(zh, (y + dy) % 8, core, x_mirror if dx else x, zl)

    def remote(src, dst, send, recv, device):
        return pltpu.make_async_remote_copy(
            src_ref=src, dst_ref=dst, send_sem=send, recv_sem=recv,
            device_id=device, device_id_type=MESH,
        )

    load_a = pltpu.make_async_copy(a_hbm, a_v, load_sem.at[0])
    load_b = pltpu.make_async_copy(b_hbm, b_v, load_sem.at[1])
    load_w = pltpu.make_async_copy(w_hbm, w_v, load_sem.at[2])
    load_a.start()
    load_b.start()
    load_w.start()

    barrier = pltpu.get_barrier_semaphore()
    greeted = [sibling]
    greeted += [rs_peer(dy, dzh) for dy in range(8) for dzh in range(4) if dy or dzh]
    greeted += [ag_peer(dx, dz) for dx in range(2) for dz in range(8) if dx or dz % 2]
    greeted += [out_peer(1, dy) for dy in range(8)]
    for device in greeted:
        pl.semaphore_signal(barrier, inc=1, device_id=device, device_id_type=MESH)

    load_a.wait()
    load_b.wait()
    load_w.wait()
    out_ref[...] = nn(a_v[...], w_v[...]).astype(BF16)
    pl.semaphore_wait(barrier, len(greeted))

    def columns(dy, half):
        return pl.ds(pl.multiple_of((y + dy) % 8 * BLOCK + half * HALF, HALF), HALF)

    swap_b = remote(b_v, b_s, bs_send, bs_recv, sibling)
    swap_b.start()
    swaps = {}
    for dy in Y_ORDER:
        swaps[dy] = remote(
            a_v.at[:, columns(dy, 1 - core)], a_s.at[dy], as_send.at[dy], as_recv.at[dy], sibling
        )
        swaps[dy].start()
    swap_b.wait()
    b_t = jnp.concatenate([b_v[...], b_s[...]], axis=0).astype(F32).T.astype(BF16)
    for dy in Y_ORDER:
        swaps[dy].wait()
        a_both = jnp.concatenate([a_v[:, columns(dy, core)], a_s[dy]], axis=0)
        part[dy] = nn(b_t, a_both).astype(BF16)
        for dzh in (2, 1, 3, 0):
            if dy or dzh:
                rows = pl.ds(pl.multiple_of((zh + dzh) % 4 * 32, 32), 32)
                remote(
                    part.at[dy, rows], rs_buf.at[dy * 4 + dzh], rs_send, rs_recv, rs_peer(dy, dzh)
                ).start()

    all_rs = rs_buf.at[pl.ds(1, 31)]
    remote(all_rs, all_rs, rs_send, rs_recv, sibling).wait_recv()
    total = part[0, pl.ds(pl.multiple_of(zh * 32, 32), 32), :].astype(F32)
    for slot in range(1, 32):
        total += rs_buf[slot].astype(F32)
    own_rows = pl.ds(pl.multiple_of((x % 2 * 2 + zl) * 128 + zh * 32, 32), 32)
    tile[core, own_rows, :] = total.astype(BF16)

    for dx in (1, 0):
        for dz in (4, 3, 5, 2, 6, 1, 7, 0):
            if dx or dz:
                piece = tile.at[core, own_rows]
                remote(piece, piece, ag_send, ag_recv, ag_peer(dx, dz)).start()
    all_ag = tile.at[core, pl.ds(0, 480)]
    remote(all_ag, all_ag, ag_send, ag_recv, sibling).wait_recv()
    swap_t = remote(tile.at[core], tile.at[core], th_send, th_recv, sibling)
    swap_t.start()
    swap_t.wait()

    @pl.when(core == 0)
    def _():
        u_ref[0:HALF, :] = tile[0].T
        u_ref[HALF:BLOCK, :] = tile[1].T

    @pl.when(core == 1)
    def _():
        u_ref[:, 0:HALF] = tile[0]
        u_ref[:, HALF:BLOCK] = tile[1]

    diagonal = lax.broadcasted_iota(jnp.int32, (BLOCK, BLOCK), 0) == lax.broadcasted_iota(
        jnp.int32, (BLOCK, BLOCK), 1
    )
    t0[...] = nt(u_ref[...], u_ref[...])
    trace = jnp.sum(jnp.where(diagonal, t0[...], 0.0), keepdims=True)
    shift = DAMPING * trace / BLOCK
    m0[...] = t0[...] + jnp.where(diagonal, shift, 0.0)
    norm = jnp.sqrt(jnp.sum(m0[...] * m0[...], keepdims=True))
    m0[...] = m0[...] * (1.0 / norm)
    b0[...] = m0[...].astype(BF16)

    def newton(m, m_half, m_next):
        e = (nn(m_half[...], m_half[...]) * 0.0625 - 0.625 * m[...]).astype(BF16)
        b1[...] = e
        t0[...] = 1.5625 * m[...] + nn(b1[...], m_half[...])
        xr[...] = t0[...].astype(BF16)
        m_next[...] = 1.5625 * t0[...] + nn(b1[...], xr[...])

    newton(m0, b0, m1)
    u1 = m1[...].astype(BF16)
    m0[...] = nn(b0[...], u1) * 0.0625 - 0.3125 * (m0[...] + m1[...])
    b0[...] = u1
    newton(m1, b0, m2)
    b0[...] = m0[...].astype(BF16)
    b1[...] = m2[...].astype(BF16)
    root = 1.25 * m0[...] - 0.390625 * m2[...] - 0.25 * nn(b0[...], b1[...])
    root = root + jnp.where(diagonal, 1.953125, 0.0)
    xr[...] = (root * lax.rsqrt(jnp.sqrt(norm))).astype(BF16)

    give_half = remote(hbuf, hbuf, ex_send, ex_recv, sibling)
    give_root = remote(xr.at[:, pl.ds(0, HALF)], rbuf, ex_send, ex_recv, sibling)

    @pl.when(core == 0)
    def _():
        for slot, x_ in ((0, x), (1, x_mirror)):
            rows = pl.ds(pl.multiple_of((x_ * 2 + zl) * 64, 64), 64)
            hbuf[slot * 64 : slot * 64 + 64, :] = nn(xr[rows, :], u_ref[...]).astype(BF16)
        give_half.start()
        give_half.wait_send()
        give_root.wait_recv()

    @pl.when(core == 1)
    def _():
        give_root.start()
        rbuf[...] = xr[:, HALF:BLOCK]
        give_root.wait_send()
        give_half.wait_recv()

    piece = (nn(hbuf[...], rbuf[...]) * math.sqrt(BLOCK)).astype(BF16)
    osrc[0] = piece[0:64]
    osrc[1] = piece[64:128]
    place = c * 8 + y
    for dy in Y_ORDER:
        for dx in (1, 0):
            if dx or dy:
                remote(
                    osrc.at[dx], oland.at[core, place], o_send, o_recv, out_peer(dx, dy)
                ).start()
    oland[core, place] = osrc[0]
    all_out = oland.at[core, pl.ds(0, 15)]
    remote(all_out, all_out, o_send, o_recv, sibling).wait_recv()
    swap_o = remote(oland.at[core], oland.at[core], of_send, of_recv, sibling)
    swap_o.start()

    def finish(half, cb):
        return pltpu.make_async_copy(
            oland.at[half, pl.ds(cb * 8, 8)],
            upd_hbm.at[:, :, pl.ds(pl.multiple_of(cb * BLOCK + half * HALF, HALF), HALF)],
            fin_sem.at[half, cb],
        )

    finish(core, 0).start()
    finish(core, 1).start()
    swap_o.wait()
    finish(1 - core, 0).start()
    finish(1 - core, 1).start()

    remote(all_rs, all_rs, rs_send, rs_recv, sibling).wait_send()
    remote(all_ag, all_ag, ag_send, ag_recv, sibling).wait_send()
    remote(all_out, all_out, o_send, o_recv, sibling).wait_send()
    for half in range(2):
        for cb in range(2):
            finish(half, cb).wait()


def on_device(inputs, weight, cotangent):
    anywhere = pl.BlockSpec(memory_space=pl.ANY)
    square = (BLOCK, BLOCK)
    dma = pltpu.SemaphoreType.DMA
    return pl.pallas_call(
        kernel,
        out_shape=(
            jax.ShapeDtypeStruct((128, 128), BF16),
            jax.ShapeDtypeStruct((8, 64, CB * BLOCK), BF16),
        ),
        in_specs=[anywhere] * 3,
        out_specs=(pl.BlockSpec(memory_space=pltpu.VMEM), anywhere),
        scratch_shapes=[
            pltpu.VMEM((128, D), BF16),
            pltpu.VMEM((D, 128), BF16),
            pltpu.VMEM((128, 128), BF16),
            pltpu.VMEM((8, 128, HALF), BF16),
            pltpu.VMEM((128, 128), BF16),
            pltpu.VMEM((8, 128, HALF), BF16),
            pltpu.VMEM((32, 32, HALF), BF16),
            pltpu.VMEM((2, BLOCK, HALF), BF16),
            pltpu.VMEM(square, BF16),
            pltpu.VMEM(square, F32),
            pltpu.VMEM(square, F32),
            pltpu.VMEM(square, F32),
            pltpu.VMEM(square, F32),
            pltpu.VMEM(square, BF16),
            pltpu.VMEM(square, BF16),
            pltpu.VMEM(square, BF16),
            pltpu.VMEM((128, BLOCK), BF16),
            pltpu.VMEM((BLOCK, HALF), BF16),
            pltpu.VMEM((2, 64, HALF), BF16),
            pltpu.VMEM((2, 16, 64, HALF), BF16),
            dma((3,)),
            dma((8,)), dma((8,)),
            dma, dma,
            dma, dma,
            dma, dma,
            dma, dma,
            dma, dma,
            dma, dma,
            dma, dma,
            dma((2, 2)),
        ],
        compiler_params=pltpu.CompilerParams(
            collective_id=0, has_side_effects=True, vmem_limit_bytes=48 * 2**20
        ),
    )(inputs, weight, cotangent)


def solution(mesh):
    placed = (P("dp", None), P(None, "pre"), P("dp", "pre"))
    return jax.shard_map(
        on_device,
        mesh=mesh,
        in_specs=placed,
        out_specs=(P("dp", "pre"), P(None, "pre", None)),
        check_vma=False,
    )
```

time: 960 us -> 72.9 us (0.08)
  waiting for transfers between devices: 873 us -> 0 us
  Pallas kernels: 0 us -> 67.2 us
  matrix products: 34.5 us -> 0 us
  blocking collectives: 24.3 us -> 0 us
  between operations: 14.3 us -> 0.65 us
    psum x1 -> x0, waiting for transfers between devices: 566 us -> none  [on_device(): gradient = lax.psum(partial_value, 'dp')]
    all_gather x5 -> x0, waiting for transfers between devices: 307 us -> none  [the longest x3 167 us: on_device(): full_state = lax.all_gather(state_rows, 'pre', axis=1, tiled=True)]
    pallas_call x0 -> x1, Pallas kernels: none -> 67.2 us  [on_device(): pl.pallas_call(kernel, out_shape=(jax.ShapeDtypeStruct((128, 128), BF16),...]
    dot_general x14 -> x0, matrix products: 34.5 us -> none  [the longest x9 25.6 us: batch_dot(): jnp.einsum('sij,sjk->sik', former, latter, precision=HIGH, preferred_elem...]
    all_gather x1 -> x0, blocking collectives: 24.3 us -> none  [on_device(): right_full = lax.all_gather(root_half[:, 1], 'pre', axis=1, tiled=True)]
  transfers between devices with their start and end apart: 6 -> 0, of which waited for: 6 -> 0; matrix products, arithmetic and copies ran while one was open for 1% -> 0% of each run, Pallas kernels for 0% -> 0%
where the time goes in v1:
time: 72.9 us; the launch traced here: 72.6 us
  Pallas kernels  67.2 us (92%)
  local copies, waits for them, and re-layouts  4.79 us (7%)
    pallas_call x1, Pallas kernels, on_device(): pl.pallas_call(kernel, out_shape=(jax.ShapeDtypeStruct((128, 128), BF16),...  67.2 us
    unnamed x8, local copies, waits for them, and re-layouts  4.79 us

profile of v1, /device:TPU:1, one launch (start us, length us, event | category | flops | bytes accessed | tf_op | source)
XLA Modules:
  0.0 72.6 jit_solution(14154923912846423329)
XLA Ops:
  0.6 0.0 copy-start
  0.6 1.2 %copy-done = bf16[128,4096]{1,0:T(8,128)(2,1)S(1)} copy-done((bf16[128,4096]{1,0:T(8,128)(2,1)S(1)}, bf16[128,4096]{1,0:T(8,128)(2,1)}, u32[]{:S(2)}) %copy-start) | copy-done | bytes 1048600
  1.9 0.0 copy-start.1
  1.9 1.2 %copy-done.1 = bf16[4096,128]{1,0:T(8,128)(2,1)S(1)} copy-done((bf16[4096,128]{1,0:T(8,128)(2,1)S(1)}, bf16[4096,128]{1,0:T(8,128)(2,1)}, u32[]{:S(2)}) %copy-start.1) | copy-done | bytes 1048600
  3.1 0.0 copy-start.2
  3.1 0.8 %copy-done.2 = bf16[128,128]{1,0:T(8,128)(2,1)S(1)} copy-done((bf16[128,128]{1,0:T(8,128)(2,1)S(1)}, bf16[128,128]{1,0:T(8,128)(2,1)}, u32[]{:S(2)}) %copy-start.2) | copy-done | bytes 32792
  3.8 67.2 %shard_map.50 = (bf16[128,128]{1,0:T(8,128)(2,1)S(1)}, bf16[8,64,1024]{2,1,0:T(8,128)(2,1)S(1)}) custom-call(bf16[128,4096]{1,0:T(8,128)(2,1)S(1)} %copy-done, bf16[4096,128]{1,0:T(8,128)(2,1)S(1)} %copy-done.1, bf16[128,128]{1,0:T(8,128)(2,1)S(1)} %copy-done.2), custom_call_target="tpu_custom_call" | custom-call | tf_op jit(solution)/shard_map/pallas_call | solution.py:231
  71.0 0.6 copy.7
  71.6 1.0 %copy.8 = bf16[8,64,1024]{2,1,0:T(8,128)(2,1)} copy(bf16[8,64,1024]{2,1,0:T(8,128)(2,1)S(1)} %get-tuple-element.5) | data formatting | bytes 2097152
Async XLA Ops:
  0.6 1.2 %copy-start = (bf16[128,4096]{1,0:T(8,128)(2,1)S(1)}, bf16[128,4096]{1,0:T(8,128)(2,1)}, u32[]{:S(2)}) copy-start(bf16[128,4096]{1,0:T(8,128)(2,1)} %a_hbm.1) | copy-start | bytes 3145732
  1.9 1.2 %copy-start.1 = (bf16[4096,128]{1,0:T(8,128)(2,1)S(1)}, bf16[4096,128]{1,0:T(8,128)(2,1)}, u32[]{:S(2)}) copy-start(bf16[4096,128]{1,0:T(8,128)(2,1)} %w_hbm.1) | copy-start | bytes 3145732
  3.1 0.8 %copy-start.2 = (bf16[128,128]{1,0:T(8,128)(2,1)S(1)}, bf16[128,128]{1,0:T(8,128)(2,1)}, u32[]{:S(2)}) copy-start(bf16[128,128]{1,0:T(8,128)(2,1)} %b_hbm.1) | copy-start | bytes 98308

commit v2 on v1

--- a/solution.py
+++ b/solution.py
@@ -28,12 +28,12 @@
 
 
 def kernel(
-    a_hbm, w_hbm, b_hbm, out_ref, upd_hbm,
+    a_hbm, w_hbm, b_hbm, out_ref, upd_ref,
     a_v, w_v, b_v, a_s, b_s, part, rs_buf, tile, u_ref,
-    m0, m1, m2, t0, b0, b1, xr, hbuf, rbuf, osrc, oland,
+    m0, m1, m2, t0, b0, b1, xr, hbuf, rbuf, osrc,
     load_sem, as_send, as_recv, bs_send, bs_recv, rs_send, rs_recv,
     ag_send, ag_recv, th_send, th_recv, ex_send, ex_recv,
-    o_send, o_recv, of_send, of_recv, fin_sem,
+    o_send, o_recv, of_send, of_recv,
 ):
     dp = lax.axis_index("dp")
     pre = lax.axis_index("pre")
@@ -82,8 +82,6 @@
 
     load_a.wait()
     load_b.wait()
-    load_w.wait()
-    out_ref[...] = nn(a_v[...], w_v[...]).astype(BF16)
     pl.semaphore_wait(barrier, len(greeted))
 
     def columns(dy, half):
@@ -110,6 +108,9 @@
                     part.at[dy, rows], rs_buf.at[dy * 4 + dzh], rs_send, rs_recv, rs_peer(dy, dzh)
                 ).start()
 
+    load_w.wait()
+    out_ref[...] = nn(a_v[...], w_v[...]).astype(BF16)
+
     all_rs = rs_buf.at[pl.ds(1, 31)]
     remote(all_rs, all_rs, rs_send, rs_recv, sibling).wait_recv()
     total = part[0, pl.ds(pl.multiple_of(zh * 32, 32), 32), :].astype(F32)
@@ -187,45 +188,52 @@
         give_root.wait_send()
         give_half.wait_recv()
 
+    def place(row_block, cb):
+        lanes = pl.ds(pl.multiple_of(cb * BLOCK + core * HALF, HALF), HALF)
+        return upd_ref.at[row_block, :, lanes]
+
+    def landing(dx, dy):
+        return place((y + 8 - dy) % 8, 1 - c if dx else c)
+
+    def give(dx, dy):
+        remote(osrc.at[dx], place(y, c), o_send, o_recv.at[dx, dy], out_peer(dx, dy)).start()
+
+    def take(dx, dy):
+        landed = landing(dx, dy)
+        remote(landed, landed, o_send, o_recv.at[dx, dy], sibling).wait_recv()
+        remote(landed, landed, of_send, of_recv, sibling).start()
+
+    def hand_on(dx, dy, step):
+        landed = landing(dx, dy)
+        remote(
+            landed, landed, o_send, o_recv.at[dx, (dy + step) % 8], out_peer(0, step % 8)
+        ).start()
+
     piece = (nn(hbuf[...], rbuf[...]) * math.sqrt(BLOCK)).astype(BF16)
     osrc[0] = piece[0:64]
     osrc[1] = piece[64:128]
-    place = c * 8 + y
-    for dy in Y_ORDER:
-        for dx in (1, 0):
-            if dx or dy:
-                remote(
-                    osrc.at[dx], oland.at[core, place], o_send, o_recv, out_peer(dx, dy)
-                ).start()
-    oland[core, place] = osrc[0]
-    all_out = oland.at[core, pl.ds(0, 15)]
-    remote(all_out, all_out, o_send, o_recv, sibling).wait_recv()
-    swap_o = remote(oland.at[core], oland.at[core], of_send, of_recv, sibling)
-    swap_o.start()
-
-    def finish(half, cb):
-        return pltpu.make_async_copy(
-            oland.at[half, pl.ds(cb * 8, 8)],
-            upd_hbm.at[:, :, pl.ds(pl.multiple_of(cb * BLOCK + half * HALF, HALF), HALF)],
-            fin_sem.at[half, cb],
-        )
-
-    finish(core, 0).start()
-    finish(core, 1).start()
-    swap_o.wait()
-    finish(1 - core, 0).start()
-    finish(1 - core, 1).start()
-
+    for dx, dy in ((1, 2), (1, 6), (0, 2), (0, 6), (1, 1), (1, 7), (0, 1), (0, 7), (1, 0)):
+        give(dx, dy)
+    remote(osrc.at[0], place(y, c), of_send, of_recv, sibling).start()
+    place(y, c)[...] = osrc[0]
+    for dx, dy, step in ((0, 2, 1), (0, 6, -1), (1, 2, 1), (1, 6, -1)):
+        take(dx, dy)
+        if dx == (dy == 6):
+            hand_on(dx, dy, 2 * step)
+        hand_on(dx, dy, step)
+    for dx, dy in ((1, 0), (0, 1), (0, 7), (1, 1), (1, 7), (0, 3), (0, 5), (0, 4), (1, 3), (1, 5), (1, 4)):
+        take(dx, dy)
+    all_half = upd_ref.at[pl.ds(0, 4)]
+    remote(all_half, all_half, of_send, of_recv, sibling).wait()
+
+    all_out = tile.at[0, pl.ds(0, 480)]
     remote(all_rs, all_rs, rs_send, rs_recv, sibling).wait_send()
     remote(all_ag, all_ag, ag_send, ag_recv, sibling).wait_send()
-    remote(all_out, all_out, o_send, o_recv, sibling).wait_send()
-    for half in range(2):
-        for cb in range(2):
-            finish(half, cb).wait()
+    remote(all_out, all_out, o_send, th_recv, sibling).wait_send()
+    remote(all_out, all_out, o_send, th_recv, sibling).wait_send()
 
 
 def on_device(inputs, weight, cotangent):
-    anywhere = pl.BlockSpec(memory_space=pl.ANY)
     square = (BLOCK, BLOCK)
     dma = pltpu.SemaphoreType.DMA
     return pl.pallas_call(
@@ -234,8 +242,8 @@
             jax.ShapeDtypeStruct((128, 128), BF16),
             jax.ShapeDtypeStruct((8, 64, CB * BLOCK), BF16),
         ),
-        in_specs=[anywhere] * 3,
-        out_specs=(pl.BlockSpec(memory_space=pltpu.VMEM), anywhere),
+        in_specs=[pl.BlockSpec(memory_space=pltpu.HBM)] * 3,
+        out_specs=(pl.BlockSpec(memory_space=pltpu.VMEM),) * 2,
         scratch_shapes=[
             pltpu.VMEM((128, D), BF16),
             pltpu.VMEM((D, 128), BF16),
@@ -256,7 +264,6 @@
             pltpu.VMEM((128, BLOCK), BF16),
             pltpu.VMEM((BLOCK, HALF), BF16),
             pltpu.VMEM((2, 64, HALF), BF16),
-            pltpu.VMEM((2, 16, 64, HALF), BF16),
             dma((3,)),
             dma((8,)), dma((8,)),
             dma, dma,
@@ -264,14 +271,13 @@
             dma, dma,
             dma, dma,
             dma, dma,
-            dma, dma,
-            dma, dma,
-            dma((2, 2)),
+            dma, dma((2, 8)),
+            dma, dma,
         ],
         compiler_params=pltpu.CompilerParams(
             collective_id=0, has_side_effects=True, vmem_limit_bytes=48 * 2**20
         ),
-    )(inputs, weight, cotangent)
+    )(*(pltpu.with_memory_space_constraint(v, pltpu.HBM) for v in (inputs, weight, cotangent)))
 
 
 def solution(mesh):

time: 72.9 us -> 64.5 us (0.88)
  Pallas kernels: 67.2 us -> 62.1 us
  local copies, waits for them, and re-layouts: 4.79 us -> 1.59 us
    pallas_call x1, Pallas kernels: 67.2 us -> 62.1 us  [on_device(): pl.pallas_call(kernel, out_shape=(jax.ShapeDtypeStruct((128, 128), BF16),...]
    unnamed x8 -> x2, local copies, waits for them, and re-layouts: 4.79 us -> 1.59 us
where the time goes in v2:
time: 64.5 us; the launch traced here: 64.3 us
  Pallas kernels  62.1 us (96%)
  local copies, waits for them, and re-layouts  1.59 us (2%)
    pallas_call x1, Pallas kernels, on_device(): pl.pallas_call(kernel, out_shape=(jax.ShapeDtypeStruct((128, 128), BF16),...  62.1 us
    unnamed x2, local copies, waits for them, and re-layouts  1.59 us

profile of v2, /device:TPU:1, one launch (start us, length us, event | category | flops | bytes accessed | tf_op | source)
XLA Modules:
  0.0 64.3 jit_solution(17313579366150222002)
XLA Ops:
  0.6 62.1 %shard_map.50 = (bf16[128,128]{1,0:T(8,128)(2,1)S(1)}, bf16[8,64,1024]{2,1,0:T(8,128)(2,1)S(1)}) custom-call(bf16[128,4096]{1,0:T(8,128)(2,1)} %a_hbm.1, bf16[4096,128]{1,0:T(8,128)(2,1)} %w_hbm.1, bf16[128,128]{1,0:T(8,128)(2,1)} %b_hbm.1), custom_call_target="tpu_custom_call" | custom-call | tf_op jit(solution)/shard_map/pallas_call | solution.py:239
  62.7 0.6 copy.7
  63.4 1.0 %copy.8 = bf16[8,64,1024]{2,1,0:T(8,128)(2,1)} copy(bf16[8,64,1024]{2,1,0:T(8,128)(2,1)S(1)} %get-tuple-element.5) | data formatting | bytes 2097152

commit v3 on v2

--- a/solution.py
+++ b/solution.py
@@ -29,10 +29,11 @@
 
 def kernel(
     a_hbm, w_hbm, b_hbm, out_ref, upd_ref,
-    a_v, w_v, b_v, a_s, b_s, part, rs_buf, tile, u_ref,
+    a_v, w_v, b_v, a_s, b_s, part, y1, z1, zs, z2, y2, tile, u_ref,
     m0, m1, m2, t0, b0, b1, xr, hbuf, rbuf, osrc,
-    load_sem, as_send, as_recv, bs_send, bs_recv, rs_send, rs_recv,
-    ag_send, ag_recv, th_send, th_recv, ex_send, ex_recv,
+    load_sem, as_send, as_recv, bs_send, bs_recv,
+    y1_send, y1_recv, z1_send, z1_recv, z2_send, z2_recv, y2_send, y2_recv,
+    yg_send, yg_recv, zg_send, zg_recv, th_send, th_recv, ex_send, ex_recv,
     o_send, o_recv, of_send, of_recv,
 ):
     dp = lax.axis_index("dp")
@@ -49,8 +50,11 @@
 
     sibling = dev(zh, y, 1 - core, x, zl)
 
-    def rs_peer(dy, dzh):
-        return dev((zh + dzh) % 4, (y + dy) % 8, core, x, zl)
+    def y_peer(dy):
+        return dev(zh, (y + dy) % 8, core, x, zl)
+
+    def z_peer(dzh):
+        return dev((zh + dzh) % 4, y, core, x, zl)
 
     def ag_peer(dx, dz):
         z_ = (z + dz) % 8
@@ -74,8 +78,8 @@
 
     barrier = pltpu.get_barrier_semaphore()
     greeted = [sibling]
-    greeted += [rs_peer(dy, dzh) for dy in range(8) for dzh in range(4) if dy or dzh]
-    greeted += [ag_peer(dx, dz) for dx in range(2) for dz in range(8) if dx or dz % 2]
+    greeted += [y_peer(dy) for dy in range(1, 8)]
+    greeted += [ag_peer(dx, dz) for dx in range(2) for dz in range(8) if dx or dz]
     greeted += [out_peer(1, dy) for dy in range(8)]
     for device in greeted:
         pl.semaphore_signal(barrier, inc=1, device_id=device, device_id_type=MESH)
@@ -97,48 +101,87 @@
         swaps[dy].start()
     swap_b.wait()
     b_t = jnp.concatenate([b_v[...], b_s[...]], axis=0).astype(F32).T.astype(BF16)
-    for dy in Y_ORDER:
+    b_t = jnp.concatenate(
+        [b_t[h * 32 + path * 16 : h * 32 + path * 16 + 16] for path in range(2) for h in range(4)],
+        axis=0,
+    )
+    for i, dy in enumerate(Y_ORDER):
         swaps[dy].wait()
         a_both = jnp.concatenate([a_v[:, columns(dy, core)], a_s[dy]], axis=0)
-        part[dy] = nn(b_t, a_both).astype(BF16)
-        for dzh in (2, 1, 3, 0):
-            if dy or dzh:
-                rows = pl.ds(pl.multiple_of((zh + dzh) % 4 * 32, 32), 32)
+        part[i] = nn(b_t, a_both).astype(BF16).reshape(2, 4, 16, HALF)
+        if dy:
+            remote(part.at[i, 0], y1.at[i], y1_send, y1_recv, y_peer(dy)).start()
+        if i % 4 == 3:
+            some = pl.ds(i - 3, 4)
+            for dzh in (2, 1, 3):
                 remote(
-                    part.at[dy, rows], rs_buf.at[dy * 4 + dzh], rs_send, rs_recv, rs_peer(dy, dzh)
+                    part.at[some, 1, (zh + dzh) % 4], z1.at[dzh - 1, some],
+                    z1_send, z1_recv, z_peer(dzh),
                 ).start()
 
     load_w.wait()
     out_ref[...] = nn(a_v[...], w_v[...]).astype(BF16)
 
-    all_rs = rs_buf.at[pl.ds(1, 31)]
-    remote(all_rs, all_rs, rs_send, rs_recv, sibling).wait_recv()
-    total = part[0, pl.ds(pl.multiple_of(zh * 32, 32), 32), :].astype(F32)
-    for slot in range(1, 32):
-        total += rs_buf[slot].astype(F32)
-    own_rows = pl.ds(pl.multiple_of((x % 2 * 2 + zl) * 128 + zh * 32, 32), 32)
-    tile[core, own_rows, :] = total.astype(BF16)
-
+    remote(z1, z1, z1_send, z1_recv, sibling).wait_recv()
+    for i, dy in enumerate(Y_ORDER):
+        terms = part[i, 1, zh].astype(F32)
+        for dzh in range(3):
+            terms += z1[dzh, i].astype(F32)
+        zs[i] = terms.astype(BF16)
+        if dy:
+            remote(zs.at[i], z2.at[i], z2_send, z2_recv, y_peer(dy)).start()
+    remote(y1, y1, y1_send, y1_recv, sibling).wait_recv()
+    total = part[7, 0].astype(F32)
+    for i in range(7):
+        total += y1[i].astype(F32)
+    y2[zh] = total.astype(BF16)
+    for dzh in (2, 1, 3):
+        remote(y2.at[zh], y2.at[zh], y2_send, y2_recv, z_peer(dzh)).start()
+
+    mine = x % 2 * 2 + zl
+    all_z2 = z2.at[pl.ds(0, 7)]
+    remote(all_z2, all_z2, z2_send, z2_recv, sibling).wait_recv()
+    total = zs[7].astype(F32)
+    for i in range(7):
+        total += z2[i].astype(F32)
+    tile[core, mine, zh, 1] = total.astype(BF16)
+    piece = tile.at[core, mine, zh, 1]
     for dx in (1, 0):
         for dz in (4, 3, 5, 2, 6, 1, 7, 0):
             if dx or dz:
-                piece = tile.at[core, own_rows]
-                remote(piece, piece, ag_send, ag_recv, ag_peer(dx, dz)).start()
-    all_ag = tile.at[core, pl.ds(0, 480)]
-    remote(all_ag, all_ag, ag_send, ag_recv, sibling).wait_recv()
-    swap_t = remote(tile.at[core], tile.at[core], th_send, th_recv, sibling)
-    swap_t.start()
-    swap_t.wait()
+                remote(piece, piece, zg_send, zg_recv, ag_peer(dx, dz)).start()
+    three = y2.at[pl.ds(0, 3)]
+    remote(three, three, y2_send, y2_recv, sibling).wait_recv()
+    total = y2[0].astype(F32)
+    for h in range(1, 4):
+        total += y2[h].astype(F32)
+    tile[core, mine, :, 0] = total.astype(BF16)
+    piece = tile.at[core, mine, :, 0]
+    for x_, zl_ in ((x_pair, 1 - zl), (x_pair, zl), (x, 1 - zl)):
+        remote(piece, piece, yg_send, yg_recv, dev(zh, y, core, x_, zl_)).start()
+    remote(three, three, yg_send, yg_recv, sibling).wait_recv()
+    swap_y = remote(
+        tile.at[core, :, :, 0], tile.at[core, :, :, 0], th_send.at[0], th_recv.at[0], sibling
+    )
+    swap_y.start()
+    all_zg = z1.at[:, pl.ds(0, 5)]
+    remote(all_zg, all_zg, zg_send, zg_recv, sibling).wait_recv()
+    swap_z = remote(
+        tile.at[core, :, :, 1], tile.at[core, :, :, 1], th_send.at[1], th_recv.at[1], sibling
+    )
+    swap_z.start()
+    swap_y.wait()
+    swap_z.wait()
 
     @pl.when(core == 0)
     def _():
-        u_ref[0:HALF, :] = tile[0].T
-        u_ref[HALF:BLOCK, :] = tile[1].T
+        u_ref[0:HALF, :] = tile[0].reshape(BLOCK, HALF).T
+        u_ref[HALF:BLOCK, :] = tile[1].reshape(BLOCK, HALF).T
 
     @pl.when(core == 1)
     def _():
-        u_ref[:, 0:HALF] = tile[0]
-        u_ref[:, HALF:BLOCK] = tile[1]
+        u_ref[:, 0:HALF] = tile[0].reshape(BLOCK, HALF)
+        u_ref[:, HALF:BLOCK] = tile[1].reshape(BLOCK, HALF)
 
     diagonal = lax.broadcasted_iota(jnp.int32, (BLOCK, BLOCK), 0) == lax.broadcasted_iota(
         jnp.int32, (BLOCK, BLOCK), 1
@@ -226,11 +269,16 @@
     all_half = upd_ref.at[pl.ds(0, 4)]
     remote(all_half, all_half, of_send, of_recv, sibling).wait()
 
-    all_out = tile.at[0, pl.ds(0, 480)]
-    remote(all_rs, all_rs, rs_send, rs_recv, sibling).wait_send()
-    remote(all_ag, all_ag, ag_send, ag_recv, sibling).wait_send()
-    remote(all_out, all_out, o_send, th_recv, sibling).wait_send()
-    remote(all_out, all_out, o_send, th_recv, sibling).wait_send()
+    remote(y1, y1, y1_send, y1_recv, sibling).wait_send()
+    remote(z1, z1, z1_send, z1_recv, sibling).wait_send()
+    remote(all_z2, all_z2, z2_send, z2_recv, sibling).wait_send()
+    remote(three, three, y2_send, y2_recv, sibling).wait_send()
+    remote(three, three, yg_send, yg_recv, sibling).wait_send()
+    remote(all_zg, all_zg, zg_send, zg_recv, sibling).wait_send()
+    all_out = tile.at[0, pl.ds(0, 3)]
+    for _ in range(2):
+        remote(all_out, all_out, o_send, y2_recv, sibling).wait_send()
+    remote(three, three, o_send, y2_recv, sibling).wait_send()
 
 
 def on_device(inputs, weight, cotangent):
@@ -250,9 +298,13 @@
             pltpu.VMEM((128, 128), BF16),
             pltpu.VMEM((8, 128, HALF), BF16),
             pltpu.VMEM((128, 128), BF16),
-            pltpu.VMEM((8, 128, HALF), BF16),
-            pltpu.VMEM((32, 32, HALF), BF16),
-            pltpu.VMEM((2, BLOCK, HALF), BF16),
+            pltpu.VMEM((8, 2, 4, 16, HALF), BF16),
+            pltpu.VMEM((7, 4, 16, HALF), BF16),
+            pltpu.VMEM((3, 8, 16, HALF), BF16),
+            pltpu.VMEM((8, 16, HALF), BF16),
+            pltpu.VMEM((8, 16, HALF), BF16),
+            pltpu.VMEM((4, 4, 16, HALF), BF16),
+            pltpu.VMEM((2, 4, 4, 2, 16, HALF), BF16),
             pltpu.VMEM(square, BF16),
             pltpu.VMEM(square, F32),
             pltpu.VMEM(square, F32),
@@ -265,14 +317,10 @@
             pltpu.VMEM((BLOCK, HALF), BF16),
             pltpu.VMEM((2, 64, HALF), BF16),
             dma((3,)),
-            dma((8,)), dma((8,)),
-            dma, dma,
-            dma, dma,
-            dma, dma,
-            dma, dma,
-            dma, dma,
-            dma, dma((2, 8)),
-            dma, dma,
+            dma((8,)), dma((8,)), dma, dma,
+            dma, dma, dma, dma, dma, dma, dma, dma,
+            dma, dma, dma, dma, dma((2,)), dma((2,)), dma, dma,
+            dma, dma((2, 8)), dma, dma,
         ],
         compiler_params=pltpu.CompilerParams(
             collective_id=0, has_side_effects=True, vmem_limit_bytes=48 * 2**20

time: 64.5 us -> 58.5 us (0.907)
  Pallas kernels: 62.1 us -> 56.1 us
    pallas_call x1, Pallas kernels: 62.1 us -> 56.1 us  [on_device(): pl.pallas_call(kernel, out_shape=(jax.ShapeDtypeStruct((128, 128), BF16),...]
where the time goes in v3:
time: 58.5 us; the launch traced here: 58.3 us
  Pallas kernels  56.1 us (96%)
  local copies, waits for them, and re-layouts  1.59 us (3%)
  between operations  0.64 us (1%)
    pallas_call x1, Pallas kernels, on_device(): pl.pallas_call(kernel, out_shape=(jax.ShapeDtypeStruct((128, 128), BF16),...  56.1 us
    unnamed x2, local copies, waits for them, and re-layouts  1.59 us

profile of v3, /device:TPU:1, one launch (start us, length us, event | category | flops | bytes accessed | tf_op | source)
XLA Modules:
  0.0 58.3 jit_solution(10023548534519518979)
XLA Ops:
  0.6 56.1 %shard_map.50 = (bf16[128,128]{1,0:T(8,128)(2,1)S(1)}, bf16[8,64,1024]{2,1,0:T(8,128)(2,1)S(1)}) custom-call(bf16[128,4096]{1,0:T(8,128)(2,1)} %a_hbm.1, bf16[4096,128]{1,0:T(8,128)(2,1)} %w_hbm.1, bf16[128,128]{1,0:T(8,128)(2,1)} %b_hbm.1), custom_call_target="tpu_custom_call" | custom-call | tf_op jit(solution)/shard_map/pallas_call | solution.py:287
  56.7 0.6 %copy.7 = bf16[128,128]{1,0:T(8,128)(2,1)} copy(bf16[128,128]{1,0:T(8,128)(2,1)S(1)} %get-tuple-element.4) | data formatting | bytes 65536
  57.4 1.0 %copy.8 = bf16[8,64,1024]{2,1,0:T(8,128)(2,1)} copy(bf16[8,64,1024]{2,1,0:T(8,128)(2,1)S(1)} %get-tuple-element.5) | data formatting | bytes 2097152

commit v4 on v3

--- a/solution.py
+++ b/solution.py
@@ -29,8 +29,8 @@
 
 def kernel(
     a_hbm, w_hbm, b_hbm, out_ref, upd_ref,
-    a_v, w_v, b_v, a_s, b_s, part, y1, z1, zs, z2, y2, tile, u_ref,
-    m0, m1, m2, t0, b0, b1, xr, hbuf, rbuf, osrc,
+    a_v, w_v, b_v, a_s, b_s, part, part_z, y1, z1, zs, z2, y2, tile, u_ref,
+    m0, m1, m2, t0, b0, b1, b2, b3, xr, hbuf, rbuf, osrc,
     load_sem, as_send, as_recv, bs_send, bs_recv,
     y1_send, y1_recv, z1_send, z1_recv, z2_send, z2_recv, y2_send, y2_recv,
     yg_send, yg_recv, zg_send, zg_recv, th_send, th_recv, ex_send, ex_recv,
@@ -77,10 +77,10 @@
     load_w.start()
 
     barrier = pltpu.get_barrier_semaphore()
-    greeted = [sibling]
-    greeted += [y_peer(dy) for dy in range(1, 8)]
-    greeted += [ag_peer(dx, dz) for dx in range(2) for dz in range(8) if dx or dz]
-    greeted += [out_peer(1, dy) for dy in range(8)]
+    greeted = [ag_peer(dx, dz) for dz in (4, 3, 5, 2, 6, 1, 7, 0) for dx in (1, 0) if dx or dz]
+    greeted += [y_peer(dy) for dy in Y_ORDER if dy]
+    greeted += [out_peer(1, dy) for dy in (2, 6, 1, 7, 0)]
+    greeted += [sibling]
     for device in greeted:
         pl.semaphore_signal(barrier, inc=1, device_id=device, device_id_type=MESH)
 
@@ -108,14 +108,16 @@
     for i, dy in enumerate(Y_ORDER):
         swaps[dy].wait()
         a_both = jnp.concatenate([a_v[:, columns(dy, core)], a_s[dy]], axis=0)
-        part[i] = nn(b_t, a_both).astype(BF16).reshape(2, 4, 16, HALF)
+        terms = nn(b_t, a_both).astype(BF16).reshape(2, 4, 16, HALF)
+        part[i] = terms[0]
+        part_z[:, i] = terms[1]
         if dy:
-            remote(part.at[i, 0], y1.at[i], y1_send, y1_recv, y_peer(dy)).start()
-        if i % 4 == 3:
-            some = pl.ds(i - 3, 4)
-            for dzh in (2, 1, 3):
+            remote(part.at[i], y1.at[i], y1_send, y1_recv, y_peer(dy)).start()
+        if i % 2:
+            some = pl.ds(i - 1, 2)
+            for dzh in (1, 3, 2):
                 remote(
-                    part.at[some, 1, (zh + dzh) % 4], z1.at[dzh - 1, some],
+                    part_z.at[(zh + dzh) % 4, some], z1.at[dzh - 1, some],
                     z1_send, z1_recv, z_peer(dzh),
                 ).start()
 
@@ -124,14 +126,14 @@
 
     remote(z1, z1, z1_send, z1_recv, sibling).wait_recv()
     for i, dy in enumerate(Y_ORDER):
-        terms = part[i, 1, zh].astype(F32)
+        terms = part_z[zh, i].astype(F32)
         for dzh in range(3):
             terms += z1[dzh, i].astype(F32)
         zs[i] = terms.astype(BF16)
         if dy:
             remote(zs.at[i], z2.at[i], z2_send, z2_recv, y_peer(dy)).start()
     remote(y1, y1, y1_send, y1_recv, sibling).wait_recv()
-    total = part[7, 0].astype(F32)
+    total = part[7].astype(F32)
     for i in range(7):
         total += y1[i].astype(F32)
     y2[zh] = total.astype(BF16)
@@ -183,51 +185,80 @@
         u_ref[:, 0:HALF] = tile[0].reshape(BLOCK, HALF)
         u_ref[:, HALF:BLOCK] = tile[1].reshape(BLOCK, HALF)
 
-    diagonal = lax.broadcasted_iota(jnp.int32, (BLOCK, BLOCK), 0) == lax.broadcasted_iota(
-        jnp.int32, (BLOCK, BLOCK), 1
-    )
+    def eye(n):
+        return lax.broadcasted_iota(jnp.int32, (n, n), 0) == lax.broadcasted_iota(
+            jnp.int32, (n, n), 1
+        )
+
     t0[...] = nt(u_ref[...], u_ref[...])
-    trace = jnp.sum(jnp.where(diagonal, t0[...], 0.0), keepdims=True)
+    blocks = [pl.ds(128 * i, 128) for i in range(4)]
+    trace = sum(jnp.where(eye(128), t0[at, at], 0.0) for at in blocks)
+    trace = jnp.sum(trace, keepdims=True)
     shift = DAMPING * trace / BLOCK
-    m0[...] = t0[...] + jnp.where(diagonal, shift, 0.0)
-    norm = jnp.sqrt(jnp.sum(m0[...] * m0[...], keepdims=True))
-    m0[...] = m0[...] * (1.0 / norm)
-    b0[...] = m0[...].astype(BF16)
-
-    def newton(m, m_half, m_next):
-        e = (nn(m_half[...], m_half[...]) * 0.0625 - 0.625 * m[...]).astype(BF16)
-        b1[...] = e
-        t0[...] = 1.5625 * m[...] + nn(b1[...], m_half[...])
-        xr[...] = t0[...].astype(BF16)
-        m_next[...] = 1.5625 * t0[...] + nn(b1[...], xr[...])
-
-    newton(m0, b0, m1)
-    u1 = m1[...].astype(BF16)
-    m0[...] = nn(b0[...], u1) * 0.0625 - 0.3125 * (m0[...] + m1[...])
-    b0[...] = u1
-    newton(m1, b0, m2)
-    b0[...] = m0[...].astype(BF16)
-    b1[...] = m2[...].astype(BF16)
-    root = 1.25 * m0[...] - 0.390625 * m2[...] - 0.25 * nn(b0[...], b1[...])
-    root = root + jnp.where(diagonal, 1.953125, 0.0)
-    xr[...] = (root * lax.rsqrt(jnp.sqrt(norm))).astype(BF16)
-
+    energy = jnp.sum(t0[...] * t0[...], keepdims=True)
+    norm = jnp.sqrt(energy + 2.0 * shift * trace + BLOCK * shift * shift)
+    for at in blocks:
+        t0[at, at] = t0[at, at] + jnp.where(eye(128), shift, 0.0)
+    scaled = t0[...] * (1.0 / norm)
+    m0[...] = scaled
+    b0[...] = scaled.astype(BF16)
+
+    bands = [pl.ds(256 * i, 256) for i in range(BLOCK // 256)]
+
+    def newton(m, m_half, m_next, next_half):
+        for at in bands:
+            b1[at] = (nn(m_half[at], m_half[...]) * 0.0625 - 0.625 * m[at]).astype(BF16)
+        for at in bands:
+            product = 1.5625 * m[at] + nn(b1[at], m_half[...])
+            t0[at] = product
+            xr[at] = product.astype(BF16)
+        for at in bands:
+            product = 1.5625 * t0[at] + nn(b1[at], xr[...])
+            m_next[at] = product
+            next_half[at] = product.astype(BF16)
+
+    newton(m0, b0, m1, b2)
+    newton(m1, b2, m2, b3)
+
+    scale = lax.rsqrt(jnp.sqrt(norm))
     give_half = remote(hbuf, hbuf, ex_send, ex_recv, sibling)
     give_root = remote(xr.at[:, pl.ds(0, HALF)], rbuf, ex_send, ex_recv, sibling)
 
     @pl.when(core == 0)
     def _():
-        for slot, x_ in ((0, x), (1, x_mirror)):
-            rows = pl.ds(pl.multiple_of((x_ * 2 + zl) * 64, 64), 64)
-            hbuf[slot * 64 : slot * 64 + 64, :] = nn(xr[rows, :], u_ref[...]).astype(BF16)
+        starts = [pl.multiple_of((x_ * 2 + zl) * 64, 64) for x_ in (x, x_mirror)]
+
+        def slabs(ref):
+            return jnp.concatenate([ref[pl.ds(start, 64), :] for start in starts], axis=0)
+
+        g = nn(slabs(b0), b2[...]) * 0.0625 - 0.3125 * (slabs(m0) + slabs(m1))
+        root = 1.25 * g - 0.390625 * slabs(m2) - 0.25 * nn(g.astype(BF16), b3[...])
+        row = lax.broadcasted_iota(jnp.int32, (128, BLOCK), 0)
+        row = jnp.where(row < 64, row + starts[0], row + (starts[1] - 64))
+        column = lax.broadcasted_iota(jnp.int32, (128, BLOCK), 1)
+        root = (root + jnp.where(row == column, 1.953125, 0.0)) * scale
+        hbuf[...] = nn(root.astype(BF16), u_ref[...]).astype(BF16)
         give_half.start()
         give_half.wait_send()
         give_root.wait_recv()
 
     @pl.when(core == 1)
     def _():
-        give_root.start()
-        rbuf[...] = xr[:, HALF:BLOCK]
+        for at in bands:
+            g = nn(b0[at], b2[...]) * 0.0625 - 0.3125 * (m0[at] + m1[at])
+            t0[at] = g
+            b1[at] = g.astype(BF16)
+        for half in range(2):
+            at = pl.ds(half * HALF, HALF)
+            root = 1.25 * t0[:, at] - 0.390625 * m2[:, at] - 0.25 * nn(b1[...], b3[:, at])
+            t0[:, at] = root
+            t0[at, at] = t0[at, at] + jnp.where(eye(HALF), 1.953125, 0.0)
+            root = (t0[:, at] * scale).astype(BF16)
+            if half:
+                rbuf[...] = root
+            else:
+                xr[:, at] = root
+                give_root.start()
         give_root.wait_send()
         give_half.wait_recv()
 
@@ -298,7 +329,8 @@
             pltpu.VMEM((128, 128), BF16),
             pltpu.VMEM((8, 128, HALF), BF16),
             pltpu.VMEM((128, 128), BF16),
-            pltpu.VMEM((8, 2, 4, 16, HALF), BF16),
+            pltpu.VMEM((8, 4, 16, HALF), BF16),
+            pltpu.VMEM((4, 8, 16, HALF), BF16),
             pltpu.VMEM((7, 4, 16, HALF), BF16),
             pltpu.VMEM((3, 8, 16, HALF), BF16),
             pltpu.VMEM((8, 16, HALF), BF16),
@@ -310,6 +342,8 @@
             pltpu.VMEM(square, F32),
             pltpu.VMEM(square, F32),
             pltpu.VMEM(square, F32),
+            pltpu.VMEM(square, BF16),
+            pltpu.VMEM(square, BF16),
             pltpu.VMEM(square, BF16),
             pltpu.VMEM(square, BF16),
             pltpu.VMEM(square, BF16),

time: 58.5 us -> 57.5 us (0.983)
  Pallas kernels: 56.1 us -> 55.1 us
    pallas_call x1, Pallas kernels: 56.1 us -> 55.1 us  [on_device(): pl.pallas_call(kernel, out_shape=(jax.ShapeDtypeStruct((128, 128), BF16),...]
where the time goes in v4:
time: 57.5 us; the launch traced here: 57.4 us
  Pallas kernels  55.1 us (96%)
  local copies, waits for them, and re-layouts  1.59 us (3%)
  between operations  0.64 us (1%)
    pallas_call x1, Pallas kernels, on_device(): pl.pallas_call(kernel, out_shape=(jax.ShapeDtypeStruct((128, 128), BF16),...  55.1 us
    unnamed x2, local copies, waits for them, and re-layouts  1.59 us

profile of v4, /device:TPU:1, one launch (start us, length us, event | category | flops | bytes accessed | tf_op | source)
XLA Modules:
  0.0 57.4 jit_solution(16359577013227562971)
XLA Ops:
  0.6 55.1 %shard_map.50 = (bf16[128,128]{1,0:T(8,128)(2,1)S(1)}, bf16[8,64,1024]{2,1,0:T(8,128)(2,1)S(1)}) custom-call(bf16[128,4096]{1,0:T(8,128)(2,1)} %a_hbm.1, bf16[4096,128]{1,0:T(8,128)(2,1)} %w_hbm.1, bf16[128,128]{1,0:T(8,128)(2,1)} %b_hbm.1), custom_call_target="tpu_custom_call" | custom-call | tf_op jit(solution)/shard_map/pallas_call | solution.py:318
  55.8 0.6 %copy.7 = bf16[128,128]{1,0:T(8,128)(2,1)} copy(bf16[128,128]{1,0:T(8,128)(2,1)S(1)} %get-tuple-element.4) | data formatting | bytes 65536
  56.4 1.0 %copy.8 = bf16[8,64,1024]{2,1,0:T(8,128)(2,1)} copy(bf16[8,64,1024]{2,1,0:T(8,128)(2,1)S(1)} %get-tuple-element.5) | data formatting | bytes 2097152

commit v5 on v4

--- a/solution.py
+++ b/solution.py
@@ -105,85 +105,108 @@
         [b_t[h * 32 + path * 16 : h * 32 + path * 16 + 16] for path in range(2) for h in range(4)],
         axis=0,
     )
+    def send_y(half, i):
+        remote(
+            part.at[half, i], y1.at[half, i], y1_send.at[half], y1_recv.at[half], y_peer(Y_ORDER[i])
+        ).start()
+
+    def send_z(half, first, count):
+        some = pl.ds(first, count)
+        for dzh in (1, 3, 2):
+            remote(
+                part_z.at[half, (zh + dzh) % 4, some], z1.at[half, dzh - 1, some],
+                z1_send.at[half], z1_recv.at[half], z_peer(dzh),
+            ).start()
+
     for i, dy in enumerate(Y_ORDER):
         swaps[dy].wait()
         a_both = jnp.concatenate([a_v[:, columns(dy, core)], a_s[dy]], axis=0)
         terms = nn(b_t, a_both).astype(BF16).reshape(2, 4, 16, HALF)
-        part[i] = terms[0]
-        part_z[:, i] = terms[1]
+        for half in range(2):
+            part[half, i] = terms[0, :, :, half * 128 : half * 128 + 128]
+            part_z[half, :, i] = terms[1, :, :, half * 128 : half * 128 + 128]
         if dy:
-            remote(part.at[i], y1.at[i], y1_send, y1_recv, y_peer(dy)).start()
+            send_y(0, i)
         if i % 2:
-            some = pl.ds(i - 1, 2)
-            for dzh in (1, 3, 2):
-                remote(
-                    part_z.at[(zh + dzh) % 4, some], z1.at[dzh - 1, some],
-                    z1_send, z1_recv, z_peer(dzh),
-                ).start()
+            send_z(0, i - 1, 2)
+    send_z(1, 0, 8)
+    for i in range(7):
+        send_y(1, i)
 
     load_w.wait()
     out_ref[...] = nn(a_v[...], w_v[...]).astype(BF16)
 
-    remote(z1, z1, z1_send, z1_recv, sibling).wait_recv()
-    for i, dy in enumerate(Y_ORDER):
-        terms = part_z[zh, i].astype(F32)
-        for dzh in range(3):
-            terms += z1[dzh, i].astype(F32)
-        zs[i] = terms.astype(BF16)
-        if dy:
-            remote(zs.at[i], z2.at[i], z2_send, z2_recv, y_peer(dy)).start()
-    remote(y1, y1, y1_send, y1_recv, sibling).wait_recv()
-    total = part[7].astype(F32)
-    for i in range(7):
-        total += y1[i].astype(F32)
-    y2[zh] = total.astype(BF16)
-    for dzh in (2, 1, 3):
-        remote(y2.at[zh], y2.at[zh], y2_send, y2_recv, z_peer(dzh)).start()
+    for half in range(2):
+        remote(z1.at[half], z1.at[half], z1_send.at[half], z1_recv.at[half], sibling).wait_recv()
+        for i, dy in enumerate(Y_ORDER):
+            terms = part_z[half, zh, i].astype(F32)
+            for dzh in range(3):
+                terms += z1[half, dzh, i].astype(F32)
+            zs[half, i] = terms.astype(BF16)
+            if dy:
+                remote(
+                    zs.at[half, i], z2.at[half, i], z2_send.at[half], z2_recv.at[half], y_peer(dy)
+                ).start()
+        remote(y1.at[half], y1.at[half], y1_send.at[half], y1_recv.at[half], sibling).wait_recv()
+        total = part[half, 7].astype(F32)
+        for i in range(7):
+            total += y1[half, i].astype(F32)
+        y2[half, zh] = total.astype(BF16)
+        for dzh in (2, 1, 3):
+            own = y2.at[half, zh]
+            remote(own, own, y2_send.at[half], y2_recv.at[half], z_peer(dzh)).start()
 
     mine = x % 2 * 2 + zl
-    all_z2 = z2.at[pl.ds(0, 7)]
-    remote(all_z2, all_z2, z2_send, z2_recv, sibling).wait_recv()
-    total = zs[7].astype(F32)
-    for i in range(7):
-        total += z2[i].astype(F32)
-    tile[core, mine, zh, 1] = total.astype(BF16)
-    piece = tile.at[core, mine, zh, 1]
-    for dx in (1, 0):
-        for dz in (4, 3, 5, 2, 6, 1, 7, 0):
-            if dx or dz:
-                remote(piece, piece, zg_send, zg_recv, ag_peer(dx, dz)).start()
-    three = y2.at[pl.ds(0, 3)]
-    remote(three, three, y2_send, y2_recv, sibling).wait_recv()
-    total = y2[0].astype(F32)
-    for h in range(1, 4):
-        total += y2[h].astype(F32)
-    tile[core, mine, :, 0] = total.astype(BF16)
-    piece = tile.at[core, mine, :, 0]
-    for x_, zl_ in ((x_pair, 1 - zl), (x_pair, zl), (x, 1 - zl)):
-        remote(piece, piece, yg_send, yg_recv, dev(zh, y, core, x_, zl_)).start()
-    remote(three, three, yg_send, yg_recv, sibling).wait_recv()
-    swap_y = remote(
-        tile.at[core, :, :, 0], tile.at[core, :, :, 0], th_send.at[0], th_recv.at[0], sibling
-    )
-    swap_y.start()
-    all_zg = z1.at[:, pl.ds(0, 5)]
-    remote(all_zg, all_zg, zg_send, zg_recv, sibling).wait_recv()
-    swap_z = remote(
-        tile.at[core, :, :, 1], tile.at[core, :, :, 1], th_send.at[1], th_recv.at[1], sibling
-    )
-    swap_z.start()
-    swap_y.wait()
-    swap_z.wait()
+    for half in range(2):
+        all_z2 = z2.at[half, pl.ds(0, 7)]
+        remote(all_z2, all_z2, z2_send.at[half], z2_recv.at[half], sibling).wait_recv()
+        total = zs[half, 7].astype(F32)
+        for i in range(7):
+            total += z2[half, i].astype(F32)
+        tile[core, half, mine, zh, 1] = total.astype(BF16)
+        piece = tile.at[core, half, mine, zh, 1]
+        for dx in (1, 0):
+            for dz in (4, 3, 5, 2, 6, 1, 7, 0):
+                if dx or dz:
+                    remote(
+                        piece, piece, zg_send.at[half], zg_recv.at[half], ag_peer(dx, dz)
+                    ).start()
+        three = y2.at[half, pl.ds(0, 3)]
+        remote(three, three, y2_send.at[half], y2_recv.at[half], sibling).wait_recv()
+        total = y2[half, 0].astype(F32)
+        for h in range(1, 4):
+            total += y2[half, h].astype(F32)
+        tile[core, half, mine, :, 0] = total.astype(BF16)
+        piece = tile.at[core, half, mine, :, 0]
+        for x_, zl_ in ((x_pair, 1 - zl), (x_pair, zl), (x, 1 - zl)):
+            remote(
+                piece, piece, yg_send.at[half], yg_recv.at[half], dev(zh, y, core, x_, zl_)
+            ).start()
+
+    def swap_tile(half, path):
+        ref = tile.at[core, half, :, :, path]
+        return remote(ref, ref, th_send.at[half, path], th_recv.at[half, path], sibling)
+
+    for half in range(2):
+        three = y2.at[half, pl.ds(0, 3)]
+        remote(three, three, yg_send.at[half], yg_recv.at[half], sibling).wait_recv()
+        swap_tile(half, 0).start()
+        all_zg = z1.at[half, :, pl.ds(0, 5)]
+        remote(all_zg, all_zg, zg_send.at[half], zg_recv.at[half], sibling).wait_recv()
+        swap_tile(half, 1).start()
+    for half in range(2):
+        for path in range(2):
+            swap_tile(half, path).wait()
 
     @pl.when(core == 0)
     def _():
-        u_ref[0:HALF, :] = tile[0].reshape(BLOCK, HALF).T
-        u_ref[HALF:BLOCK, :] = tile[1].reshape(BLOCK, HALF).T
+        for i in range(4):
+            u_ref[i * 128 : i * 128 + 128, :] = tile[i // 2, i % 2].reshape(BLOCK, 128).T
 
     @pl.when(core == 1)
     def _():
-        u_ref[:, 0:HALF] = tile[0].reshape(BLOCK, HALF)
-        u_ref[:, HALF:BLOCK] = tile[1].reshape(BLOCK, HALF)
+        for i in range(4):
+            u_ref[:, i * 128 : i * 128 + 128] = tile[i // 2, i % 2].reshape(BLOCK, 128)
 
     def eye(n):
         return lax.broadcasted_iota(jnp.int32, (n, n), 0) == lax.broadcasted_iota(
@@ -275,6 +298,9 @@
     def take(dx, dy):
         landed = landing(dx, dy)
         remote(landed, landed, o_send, o_recv.at[dx, dy], sibling).wait_recv()
+
+    def share(dx, dy):
+        landed = landing(dx, dy)
         remote(landed, landed, of_send, of_recv, sibling).start()
 
     def hand_on(dx, dy, step):
@@ -295,21 +321,24 @@
         if dx == (dy == 6):
             hand_on(dx, dy, 2 * step)
         hand_on(dx, dy, step)
-    for dx, dy in ((1, 0), (0, 1), (0, 7), (1, 1), (1, 7), (0, 3), (0, 5), (0, 4), (1, 3), (1, 5), (1, 4)):
+        share(dx, dy)
+    for dx, dy in ((1, 0), (0, 1), (0, 7), (1, 1), (1, 7), (0, 3), (0, 5), (1, 3), (1, 5), (0, 4), (1, 4)):
         take(dx, dy)
+        share(dx, dy)
     all_half = upd_ref.at[pl.ds(0, 4)]
     remote(all_half, all_half, of_send, of_recv, sibling).wait()
 
-    remote(y1, y1, y1_send, y1_recv, sibling).wait_send()
-    remote(z1, z1, z1_send, z1_recv, sibling).wait_send()
-    remote(all_z2, all_z2, z2_send, z2_recv, sibling).wait_send()
-    remote(three, three, y2_send, y2_recv, sibling).wait_send()
-    remote(three, three, yg_send, yg_recv, sibling).wait_send()
-    remote(all_zg, all_zg, zg_send, zg_recv, sibling).wait_send()
-    all_out = tile.at[0, pl.ds(0, 3)]
-    for _ in range(2):
-        remote(all_out, all_out, o_send, y2_recv, sibling).wait_send()
-    remote(three, three, o_send, y2_recv, sibling).wait_send()
+    for half in range(2):
+        all_z2 = z2.at[half, pl.ds(0, 7)]
+        three = y2.at[half, pl.ds(0, 3)]
+        all_zg = z1.at[half, :, pl.ds(0, 5)]
+        for sent, sem in (
+            (y1.at[half], y1_send), (z1.at[half], z1_send), (all_z2, z2_send),
+            (three, y2_send), (three, yg_send), (all_zg, zg_send),
+        ):
+            remote(sent, sent, sem.at[half], th_recv.at[0, 0], sibling).wait_send()
+    for sent in (tile.at[0, 0], tile.at[0, 0], tile.at[0, 1], tile.at[0, 0, pl.ds(0, 3)]):
+        remote(sent, sent, o_send, th_recv.at[0, 0], sibling).wait_send()
 
 
 def on_device(inputs, weight, cotangent):
@@ -329,14 +358,14 @@
             pltpu.VMEM((128, 128), BF16),
             pltpu.VMEM((8, 128, HALF), BF16),
             pltpu.VMEM((128, 128), BF16),
-            pltpu.VMEM((8, 4, 16, HALF), BF16),
-            pltpu.VMEM((4, 8, 16, HALF), BF16),
-            pltpu.VMEM((7, 4, 16, HALF), BF16),
-            pltpu.VMEM((3, 8, 16, HALF), BF16),
-            pltpu.VMEM((8, 16, HALF), BF16),
-            pltpu.VMEM((8, 16, HALF), BF16),
-            pltpu.VMEM((4, 4, 16, HALF), BF16),
-            pltpu.VMEM((2, 4, 4, 2, 16, HALF), BF16),
+            pltpu.VMEM((2, 8, 4, 16, 128), BF16),
+            pltpu.VMEM((2, 4, 8, 16, 128), BF16),
+            pltpu.VMEM((2, 7, 4, 16, 128), BF16),
+            pltpu.VMEM((2, 3, 8, 16, 128), BF16),
+            pltpu.VMEM((2, 8, 16, 128), BF16),
+            pltpu.VMEM((2, 8, 16, 128), BF16),
+            pltpu.VMEM((2, 4, 4, 16, 128), BF16),
+            pltpu.VMEM((2, 2, 4, 4, 2, 16, 128), BF16),
             pltpu.VMEM(square, BF16),
             pltpu.VMEM(square, F32),
             pltpu.VMEM(square, F32),
@@ -352,8 +381,8 @@
             pltpu.VMEM((2, 64, HALF), BF16),
             dma((3,)),
             dma((8,)), dma((8,)), dma, dma,
-            dma, dma, dma, dma, dma, dma, dma, dma,
-            dma, dma, dma, dma, dma((2,)), dma((2,)), dma, dma,
+            *[dma((2,))] * 12,
+            dma((2, 2)), dma((2, 2)), dma, dma,
             dma, dma((2, 8)), dma, dma,
         ],
         compiler_params=pltpu.CompilerParams(

time: 57.5 us -> 55.8 us (0.970)
  Pallas kernels: 55.1 us -> 53.5 us
    pallas_call x1, Pallas kernels: 55.1 us -> 53.5 us  [on_device(): pl.pallas_call(kernel, out_shape=(jax.ShapeDtypeStruct((128, 128), BF16),...]
where the time goes in v5:
time: 55.8 us; the launch traced here: 55.7 us
  Pallas kernels  53.5 us (96%)
  local copies, waits for them, and re-layouts  1.59 us (3%)
  between operations  0.64 us (1%)
    pallas_call x1, Pallas kernels, on_device(): pl.pallas_call(kernel, out_shape=(jax.ShapeDtypeStruct((128, 128), BF16),...  53.5 us
    unnamed x2, local copies, waits for them, and re-layouts  1.59 us

profile of v5, /device:TPU:1, one launch (start us, length us, event | category | flops | bytes accessed | tf_op | source)
XLA Modules:
  0.0 55.7 jit_solution(4571089356603041997)
XLA Ops:
  0.6 53.5 %shard_map.50 = (bf16[128,128]{1,0:T(8,128)(2,1)S(1)}, bf16[8,64,1024]{2,1,0:T(8,128)(2,1)S(1)}) custom-call(bf16[128,4096]{1,0:T(8,128)(2,1)} %a_hbm.1, bf16[4096,128]{1,0:T(8,128)(2,1)} %w_hbm.1, bf16[128,128]{1,0:T(8,128)(2,1)} %b_hbm.1), custom_call_target="tpu_custom_call" | custom-call | tf_op jit(solution)/shard_map/pallas_call | solution.py:347
  54.1 0.6 %copy.7 = bf16[128,128]{1,0:T(8,128)(2,1)} copy(bf16[128,128]{1,0:T(8,128)(2,1)S(1)} %get-tuple-element.4) | data formatting | bytes 65536
  54.7 1.0 %copy.8 = bf16[8,64,1024]{2,1,0:T(8,128)(2,1)} copy(bf16[8,64,1024]{2,1,0:T(8,128)(2,1)S(1)} %get-tuple-element.5) | data formatting | bytes 2097152

commit v6 on v5

--- a/solution.py
+++ b/solution.py
@@ -29,20 +29,20 @@
 
 def kernel(
     a_hbm, w_hbm, b_hbm, out_ref, upd_ref,
-    a_v, w_v, b_v, a_s, b_s, part, part_z, y1, z1, zs, z2, y2, tile, u_ref,
-    m0, m1, m2, t0, b0, b1, b2, b3, xr, hbuf, rbuf, osrc,
-    load_sem, as_send, as_recv, bs_send, bs_recv,
+    a_v, w_v, b_v, give, got, kept, part, part_z, y1, z1, zs, z2, y2, tile, u_ref,
+    m0, m1, m2, t0, b0, b1, b2, b3, xr, hbuf, osrc,
+    load_sem, sw_send, sw_recv,
     y1_send, y1_recv, z1_send, z1_recv, z2_send, z2_recv, y2_send, y2_recv,
     yg_send, yg_recv, zg_send, zg_recv, th_send, th_recv, ex_send, ex_recv,
     o_send, o_recv, of_send, of_recv,
 ):
     dp = lax.axis_index("dp")
     pre = lax.axis_index("pre")
-    zh, y, core = dp // 16, (dp // 2) % 8, dp % 2
-    x, zl = pre // 2, pre % 2
+    zh, y, core = lax.div(dp, 16), lax.rem(lax.div(dp, 2), 8), lax.rem(dp, 2)
+    x, zl = lax.div(pre, 2), lax.rem(pre, 2)
     z = zh * 2 + zl
-    c = x // 2
-    x_pair = c * 2 + (1 - x % 2)
+    c = lax.div(x, 2)
+    x_pair = c * 2 + (1 - lax.rem(x, 2))
     x_mirror = 3 - x
 
     def dev(zh_, y_, core_, x_, zl_):
@@ -51,17 +51,17 @@
     sibling = dev(zh, y, 1 - core, x, zl)
 
     def y_peer(dy):
-        return dev(zh, (y + dy) % 8, core, x, zl)
+        return dev(zh, lax.rem(y + dy, 8), core, x, zl)
 
     def z_peer(dzh):
-        return dev((zh + dzh) % 4, y, core, x, zl)
+        return dev(lax.rem(zh + dzh, 4), y, core, x, zl)
 
     def ag_peer(dx, dz):
-        z_ = (z + dz) % 8
-        return dev(z_ // 2, y, core, x_pair if dx else x, z_ % 2)
+        z_ = lax.rem(z + dz, 8)
+        return dev(lax.div(z_, 2), y, core, x_pair if dx else x, lax.rem(z_, 2))
 
     def out_peer(dx, dy):
-        return dev(zh, (y + dy) % 8, core, x_mirror if dx else x, zl)
+        return dev(zh, lax.rem(y + dy, 8), core, x_mirror if dx else x, zl)
 
     def remote(src, dst, send, recv, device):
         return pltpu.make_async_remote_copy(
@@ -69,12 +69,15 @@
             device_id=device, device_id_type=MESH,
         )
 
-    load_a = pltpu.make_async_copy(a_hbm, a_v, load_sem.at[0])
-    load_b = pltpu.make_async_copy(b_hbm, b_v, load_sem.at[1])
-    load_w = pltpu.make_async_copy(w_hbm, w_v, load_sem.at[2])
-    load_a.start()
+    def load_a(i):
+        at = pl.ds(pl.multiple_of(lax.rem(y + Y_ORDER[i], 8) * BLOCK, BLOCK), BLOCK)
+        return pltpu.make_async_copy(a_hbm.at[:, at], a_v.at[:, at], load_sem.at[i])
+
+    load_b = pltpu.make_async_copy(b_hbm, b_v, load_sem.at[8])
+    load_w = pltpu.make_async_copy(w_hbm, w_v, load_sem.at[9])
     load_b.start()
-    load_w.start()
+    for i in range(8):
+        load_a(i).start()
 
     barrier = pltpu.get_barrier_semaphore()
     greeted = [ag_peer(dx, dz) for dz in (4, 3, 5, 2, 6, 1, 7, 0) for dx in (1, 0) if dx or dz]
@@ -84,27 +87,34 @@
     for device in greeted:
         pl.semaphore_signal(barrier, inc=1, device_id=device, device_id_type=MESH)
 
-    load_a.wait()
+    def columns(dy, half):
+        return pl.ds(pl.multiple_of(lax.rem(y + dy, 8) * BLOCK + half * HALF, HALF), HALF)
+
     load_b.wait()
-    pl.semaphore_wait(barrier, len(greeted))
-
-    def columns(dy, half):
-        return pl.ds(pl.multiple_of((y + dy) % 8 * BLOCK + half * HALF, HALF), HALF)
-
-    swap_b = remote(b_v, b_s, bs_send, bs_recv, sibling)
-    swap_b.start()
-    swaps = {}
-    for dy in Y_ORDER:
-        swaps[dy] = remote(
-            a_v.at[:, columns(dy, 1 - core)], a_s.at[dy], as_send.at[dy], as_recv.at[dy], sibling
-        )
-        swaps[dy].start()
-    swap_b.wait()
-    b_t = jnp.concatenate([b_v[...], b_s[...]], axis=0).astype(F32).T.astype(BF16)
+    b_t = b_v[...].astype(F32).T.astype(BF16)
     b_t = jnp.concatenate(
         [b_t[h * 32 + path * 16 : h * 32 + path * 16 + 16] for path in range(2) for h in range(4)],
         axis=0,
     )
+    for i, dy in enumerate(Y_ORDER):
+        load_a(i).wait()
+        terms = nn(b_t, a_v[:, columns(dy, 1 - core)]).astype(BF16)
+        give[0, i] = terms[:, 0:128]
+        give[1, i] = terms[:, 128:HALF]
+        kept[i] = nn(b_t, a_v[:, columns(dy, core)])
+    load_w.start()
+    pl.semaphore_wait(barrier, len(greeted))
+
+    def swap(half, pair):
+        some = pl.ds(2 * pair, 2)
+        return remote(
+            give.at[half, some], got.at[half, some], sw_send.at[half, pair], sw_recv.at[half, pair],
+            sibling,
+        )
+
+    for pair in range(4):
+        swap(0, pair).start()
+
     def send_y(half, i):
         remote(
             part.at[half, i], y1.at[half, i], y1_send.at[half], y1_recv.at[half], y_peer(Y_ORDER[i])
@@ -114,24 +124,31 @@
         some = pl.ds(first, count)
         for dzh in (1, 3, 2):
             remote(
-                part_z.at[half, (zh + dzh) % 4, some], z1.at[half, dzh - 1, some],
+                part_z.at[half, lax.rem(zh + dzh, 4), some], z1.at[half, dzh - 1, some],
                 z1_send.at[half], z1_recv.at[half], z_peer(dzh),
             ).start()
 
-    for i, dy in enumerate(Y_ORDER):
-        swaps[dy].wait()
-        a_both = jnp.concatenate([a_v[:, columns(dy, core)], a_s[dy]], axis=0)
-        terms = nn(b_t, a_both).astype(BF16).reshape(2, 4, 16, HALF)
-        for half in range(2):
-            part[half, i] = terms[0, :, :, half * 128 : half * 128 + 128]
-            part_z[half, :, i] = terms[1, :, :, half * 128 : half * 128 + 128]
-        if dy:
-            send_y(0, i)
-        if i % 2:
-            send_z(0, i - 1, 2)
-    send_z(1, 0, 8)
-    for i in range(7):
-        send_y(1, i)
+    for half in range(2):
+        for pair in range(4):
+            swap(half, pair).wait()
+            for i in (2 * pair, 2 * pair + 1):
+                lanes = pl.ds(half * 128, 128)
+                terms = (kept[i, :, lanes] + got[half, i].astype(F32)).astype(BF16)
+                terms = terms.reshape(2, 4, 16, 128)
+                part[half, i] = terms[0]
+                part_z[half, :, i] = terms[1]
+            if half == 0:
+                send_z(half, 2 * pair, 2)
+                swap(1, pair).start()
+                for i in (2 * pair, 2 * pair + 1):
+                    if Y_ORDER[i]:
+                        send_y(half, i)
+            else:
+                if pair % 2:
+                    send_z(half, 2 * pair - 2, 4)
+                for i in (2 * pair, 2 * pair + 1):
+                    if Y_ORDER[i]:
+                        send_y(half, i)
 
     load_w.wait()
     out_ref[...] = nn(a_v[...], w_v[...]).astype(BF16)
@@ -156,7 +173,7 @@
             own = y2.at[half, zh]
             remote(own, own, y2_send.at[half], y2_recv.at[half], z_peer(dzh)).start()
 
-    mine = x % 2 * 2 + zl
+    mine = lax.rem(x, 2) * 2 + zl
     for half in range(2):
         all_z2 = z2.at[half, pl.ds(0, 7)]
         remote(all_z2, all_z2, z2_send.at[half], z2_recv.at[half], sibling).wait_recv()
@@ -245,7 +262,6 @@
 
     scale = lax.rsqrt(jnp.sqrt(norm))
     give_half = remote(hbuf, hbuf, ex_send, ex_recv, sibling)
-    give_root = remote(xr.at[:, pl.ds(0, HALF)], rbuf, ex_send, ex_recv, sibling)
 
     @pl.when(core == 0)
     def _():
@@ -263,7 +279,6 @@
         hbuf[...] = nn(root.astype(BF16), u_ref[...]).astype(BF16)
         give_half.start()
         give_half.wait_send()
-        give_root.wait_recv()
 
     @pl.when(core == 1)
     def _():
@@ -276,23 +291,20 @@
             root = 1.25 * t0[:, at] - 0.390625 * m2[:, at] - 0.25 * nn(b1[...], b3[:, at])
             t0[:, at] = root
             t0[at, at] = t0[at, at] + jnp.where(eye(HALF), 1.953125, 0.0)
-            root = (t0[:, at] * scale).astype(BF16)
-            if half:
-                rbuf[...] = root
-            else:
-                xr[:, at] = root
-                give_root.start()
-        give_root.wait_send()
+            xr[:, at] = (t0[:, at] * scale).astype(BF16)
         give_half.wait_recv()
+        piece = (nn(hbuf[...], xr[...]) * math.sqrt(BLOCK)).astype(BF16)
+        osrc[0] = piece[0:64]
+        osrc[1] = piece[64:128]
 
     def place(row_block, cb):
-        lanes = pl.ds(pl.multiple_of(cb * BLOCK + core * HALF, HALF), HALF)
+        lanes = pl.ds(pl.multiple_of(cb * BLOCK, BLOCK), BLOCK)
         return upd_ref.at[row_block, :, lanes]
 
     def landing(dx, dy):
-        return place((y + 8 - dy) % 8, 1 - c if dx else c)
-
-    def give(dx, dy):
+        return place(lax.rem(y + 8 - dy, 8), 1 - c if dx else c)
+
+    def send_out(dx, dy):
         remote(osrc.at[dx], place(y, c), o_send, o_recv.at[dx, dy], out_peer(dx, dy)).start()
 
     def take(dx, dy):
@@ -309,24 +321,28 @@
             landed, landed, o_send, o_recv.at[dx, (dy + step) % 8], out_peer(0, step % 8)
         ).start()
 
-    piece = (nn(hbuf[...], rbuf[...]) * math.sqrt(BLOCK)).astype(BF16)
-    osrc[0] = piece[0:64]
-    osrc[1] = piece[64:128]
-    for dx, dy in ((1, 2), (1, 6), (0, 2), (0, 6), (1, 1), (1, 7), (0, 1), (0, 7), (1, 0)):
-        give(dx, dy)
-    remote(osrc.at[0], place(y, c), of_send, of_recv, sibling).start()
-    place(y, c)[...] = osrc[0]
-    for dx, dy, step in ((0, 2, 1), (0, 6, -1), (1, 2, 1), (1, 6, -1)):
-        take(dx, dy)
-        if dx == (dy == 6):
-            hand_on(dx, dy, 2 * step)
-        hand_on(dx, dy, step)
-        share(dx, dy)
-    for dx, dy in ((1, 0), (0, 1), (0, 7), (1, 1), (1, 7), (0, 3), (0, 5), (1, 3), (1, 5), (0, 4), (1, 4)):
-        take(dx, dy)
-        share(dx, dy)
-    all_half = upd_ref.at[pl.ds(0, 4)]
-    remote(all_half, all_half, of_send, of_recv, sibling).wait()
+    @pl.when(core == 1)
+    def _():
+        for dx, dy in ((1, 2), (1, 6), (0, 2), (0, 6), (1, 1), (1, 7), (0, 1), (0, 7), (1, 0)):
+            send_out(dx, dy)
+        remote(osrc.at[0], place(y, c), of_send, of_recv, sibling).start()
+        place(y, c)[...] = osrc[0]
+        for dx, dy, step in ((0, 2, 1), (0, 6, -1), (1, 2, 1), (1, 6, -1)):
+            take(dx, dy)
+            if dx == (dy == 6):
+                hand_on(dx, dy, 2 * step)
+            hand_on(dx, dy, step)
+            share(dx, dy)
+        for dx, dy in ((1, 0), (0, 1), (0, 7), (1, 1), (1, 7), (0, 3), (0, 5), (1, 3), (1, 5), (0, 4), (1, 4)):
+            take(dx, dy)
+            share(dx, dy)
+        for sent in [tile.at[0]] * 3 + [tile.at[0, 0], tile.at[0, 0, pl.ds(0, 2)]]:
+            remote(sent, sent, o_send, th_recv.at[0, 0], sibling).wait_send()
+        remote(upd_ref, upd_ref, of_send, of_recv, sibling).wait_send()
+
+    @pl.when(core == 0)
+    def _():
+        remote(upd_ref, upd_ref, of_send, of_recv, sibling).wait_recv()
 
     for half in range(2):
         all_z2 = z2.at[half, pl.ds(0, 7)]
@@ -337,8 +353,6 @@
             (three, y2_send), (three, yg_send), (all_zg, zg_send),
         ):
             remote(sent, sent, sem.at[half], th_recv.at[0, 0], sibling).wait_send()
-    for sent in (tile.at[0, 0], tile.at[0, 0], tile.at[0, 1], tile.at[0, 0, pl.ds(0, 3)]):
-        remote(sent, sent, o_send, th_recv.at[0, 0], sibling).wait_send()
 
 
 def on_device(inputs, weight, cotangent):
@@ -356,8 +370,9 @@
             pltpu.VMEM((128, D), BF16),
             pltpu.VMEM((D, 128), BF16),
             pltpu.VMEM((128, 128), BF16),
-            pltpu.VMEM((8, 128, HALF), BF16),
-            pltpu.VMEM((128, 128), BF16),
+            pltpu.VMEM((2, 8, 128, 128), BF16),
+            pltpu.VMEM((2, 8, 128, 128), BF16),
+            pltpu.VMEM((8, 128, HALF), F32),
             pltpu.VMEM((2, 8, 4, 16, 128), BF16),
             pltpu.VMEM((2, 4, 8, 16, 128), BF16),
             pltpu.VMEM((2, 7, 4, 16, 128), BF16),
@@ -377,10 +392,9 @@
             pltpu.VMEM(square, BF16),
             pltpu.VMEM(square, BF16),
             pltpu.VMEM((128, BLOCK), BF16),
-            pltpu.VMEM((BLOCK, HALF), BF16),
-            pltpu.VMEM((2, 64, HALF), BF16),
-            dma((3,)),
-            dma((8,)), dma((8,)), dma, dma,
+            pltpu.VMEM((2, 64, BLOCK), BF16),
+            dma((10,)),
+            dma((2, 4)), dma((2, 4)),
             *[dma((2,))] * 12,
             dma((2, 2)), dma((2, 2)), dma, dma,
             dma, dma((2, 8)), dma, dma,

time: 55.8 us -> 55 us (0.986)
  Pallas kernels: 53.5 us -> 52.7 us
    pallas_call x1, Pallas kernels: 53.5 us -> 52.7 us  [on_device(): pl.pallas_call(kernel, out_shape=(jax.ShapeDtypeStruct((128, 128), BF16),...]
where the time goes in v6:
time: 55 us; the launch traced here: 54.9 us
  Pallas kernels  52.7 us (96%)
  local copies, waits for them, and re-layouts  1.59 us (3%)
  between operations  0.64 us (1%)
    pallas_call x1, Pallas kernels, on_device(): pl.pallas_call(kernel, out_shape=(jax.ShapeDtypeStruct((128, 128), BF16),...  52.7 us
    unnamed x2, local copies, waits for them, and re-layouts  1.59 us

profile of v6, /device:TPU:1, one launch (start us, length us, event | category | flops | bytes accessed | tf_op | source)
XLA Modules:
  0.0 54.9 jit_solution(11217777065304205663)
XLA Ops:
  0.6 52.7 %shard_map.50 = (bf16[128,128]{1,0:T(8,128)(2,1)S(1)}, bf16[8,64,1024]{2,1,0:T(8,128)(2,1)S(1)}) custom-call(bf16[128,4096]{1,0:T(8,128)(2,1)} %a_hbm.1, bf16[4096,128]{1,0:T(8,128)(2,1)} %w_hbm.1, bf16[128,128]{1,0:T(8,128)(2,1)} %b_hbm.1), custom_call_target="tpu_custom_call" | custom-call | tf_op jit(solution)/shard_map/pallas_call | solution.py:361
  53.3 0.6 %copy.7 = bf16[128,128]{1,0:T(8,128)(2,1)} copy(bf16[128,128]{1,0:T(8,128)(2,1)S(1)} %get-tuple-element.4) | data formatting | bytes 65536
  53.9 1.0 %copy.8 = bf16[8,64,1024]{2,1,0:T(8,128)(2,1)} copy(bf16[8,64,1024]{2,1,0:T(8,128)(2,1)S(1)} %get-tuple-element.5) | data formatting | bytes 2097152

commit v7 on v6

--- a/solution.py
+++ b/solution.py
@@ -122,7 +122,7 @@
 
     def send_z(half, first, count):
         some = pl.ds(first, count)
-        for dzh in (1, 3, 2):
+        for dzh in (2, 1, 3):
             remote(
                 part_z.at[half, lax.rem(zh + dzh, 4), some], z1.at[half, dzh - 1, some],
                 z1_send.at[half], z1_recv.at[half], z_peer(dzh),
@@ -182,8 +182,8 @@
             total += z2[half, i].astype(F32)
         tile[core, half, mine, zh, 1] = total.astype(BF16)
         piece = tile.at[core, half, mine, zh, 1]
-        for dx in (1, 0):
-            for dz in (4, 3, 5, 2, 6, 1, 7, 0):
+        for dz in (4, 3, 5, 2, 6, 1, 7, 0):
+            for dx in (1, 0):
                 if dx or dz:
                     remote(
                         piece, piece, zg_send.at[half], zg_recv.at[half], ag_peer(dx, dz)
@@ -355,14 +355,23 @@
             remote(sent, sent, sem.at[half], th_recv.at[0, 0], sibling).wait_send()
 
 
+def drain(out_vmem, upd_vmem, out_hbm, upd_hbm, sem):
+    copies = [pltpu.make_async_copy(out_vmem, out_hbm, sem.at[8])]
+    copies += [pltpu.make_async_copy(upd_vmem.at[i], upd_hbm.at[i], sem.at[i]) for i in range(8)]
+    for copy in copies:
+        copy.start()
+    for copy in copies:
+        copy.wait()
+
+
 def on_device(inputs, weight, cotangent):
     square = (BLOCK, BLOCK)
     dma = pltpu.SemaphoreType.DMA
-    return pl.pallas_call(
+    results = pl.pallas_call(
         kernel,
         out_shape=(
-            jax.ShapeDtypeStruct((128, 128), BF16),
-            jax.ShapeDtypeStruct((8, 64, CB * BLOCK), BF16),
+            pltpu.VMEM((128, 128), BF16),
+            pltpu.VMEM((8, 64, CB * BLOCK), BF16),
         ),
         in_specs=[pl.BlockSpec(memory_space=pltpu.HBM)] * 3,
         out_specs=(pl.BlockSpec(memory_space=pltpu.VMEM),) * 2,
@@ -403,6 +412,16 @@
             collective_id=0, has_side_effects=True, vmem_limit_bytes=48 * 2**20
         ),
     )(*(pltpu.with_memory_space_constraint(v, pltpu.HBM) for v in (inputs, weight, cotangent)))
+    return pl.pallas_call(
+        drain,
+        out_shape=(
+            jax.ShapeDtypeStruct((128, 128), BF16),
+            jax.ShapeDtypeStruct((8, 64, CB * BLOCK), BF16),
+        ),
+        in_specs=[pl.BlockSpec(memory_space=pltpu.VMEM)] * 2,
+        out_specs=(pl.BlockSpec(memory_space=pl.ANY),) * 2,
+        scratch_shapes=[dma((9,))],
+    )(*(pltpu.with_memory_space_constraint(v, pltpu.VMEM) for v in results))
 
 
 def solution(mesh):

time: 55 us -> 54.2 us (0.985)
  local copies, waits for them, and re-layouts: 1.59 us -> 0 us
  Pallas kernels: 52.7 us -> 53.4 us
    unnamed x2 -> x0, local copies, waits for them, and re-layouts: 1.59 us -> none
    pallas_call x1 -> x2, Pallas kernels: 52.7 us -> 53.4 us  [the longest x1 52.3 us: on_device(): pl.pallas_call(kernel, out_shape=(pltpu.VMEM((128, 128), BF16), pltpu.VME...]
where the time goes in v7:
time: 54.2 us; the launch traced here: 54 us
  Pallas kernels  53.4 us (99%)
  between operations  0.64 us (1%)
    pallas_call x1, Pallas kernels, on_device(): pl.pallas_call(kernel, out_shape=(pltpu.VMEM((128, 128), BF16), pltpu.VME...  52.3 us

profile of v7, /device:TPU:1, one launch (start us, length us, event | category | flops | bytes accessed | tf_op | source)
XLA Modules:
  0.0 54.0 jit_solution(1178981975065615632)
XLA Ops:
  0.6 52.3 %shard_map.50 = (bf16[128,128]{1,0:T(8,128)(2,1)S(1)}, bf16[8,64,1024]{2,1,0:T(8,128)(2,1)S(1)}) custom-call(bf16[128,4096]{1,0:T(8,128)(2,1)} %a_hbm.1, bf16[4096,128]{1,0:T(8,128)(2,1)} %w_hbm.1, bf16[128,128]{1,0:T(8,128)(2,1)} %b_hbm.1), custom_call_target="tpu_custom_call" | custom-call | tf_op jit(solution)/shard_map/pallas_call | solution.py:370
  53.0 1.0 %shard_map.51 = (bf16[128,128]{1,0:T(8,128)(2,1)}, bf16[8,64,1024]{2,1,0:T(8,128)(2,1)}) custom-call(bf16[128,128]{1,0:T(8,128)(2,1)S(1)} %get-tuple-element.4.out_vmem, bf16[8,64,1024]{2,1,0:T(8,128)(2,1)S(1)} %get-tuple-element.5.upd_vmem), custom_call_target="tpu_custom_call" | custom-call | tf_op jit(solution)/shard_map/pallas_call | solution.py:415

commit v8 on v7

--- a/solution.py
+++ b/solution.py
@@ -245,9 +245,11 @@
 
     bands = [pl.ds(256 * i, 256) for i in range(BLOCK // 256)]
 
-    def newton(m, m_half, m_next, next_half):
+    def square(m, m_half):
         for at in bands:
             b1[at] = (nn(m_half[at], m_half[...]) * 0.0625 - 0.625 * m[at]).astype(BF16)
+
+    def fifth(m, m_half, m_next, next_half):
         for at in bands:
             product = 1.5625 * m[at] + nn(b1[at], m_half[...])
             t0[at] = product
@@ -257,8 +259,9 @@
             m_next[at] = product
             next_half[at] = product.astype(BF16)
 
-    newton(m0, b0, m1, b2)
-    newton(m1, b2, m2, b3)
+    square(m0, b0)
+    fifth(m0, b0, m1, b2)
+    square(m1, b2)
 
     scale = lax.rsqrt(jnp.sqrt(norm))
     give_half = remote(hbuf, hbuf, ex_send, ex_recv, sibling)
@@ -270,8 +273,12 @@
         def slabs(ref):
             return jnp.concatenate([ref[pl.ds(start, 64), :] for start in starts], axis=0)
 
+        e = slabs(b1).astype(F32)
         g = nn(slabs(b0), b2[...]) * 0.0625 - 0.3125 * (slabs(m0) + slabs(m1))
-        root = 1.25 * g - 0.390625 * slabs(m2) - 0.25 * nn(g.astype(BF16), b3[...])
+        once = 1.5625 * (g + e) + nn(g.astype(BF16), b1[...])
+        twice = 2.44140625 * e + 1.5625 * once + nn(once.astype(BF16), b1[...])
+        last = 3.814697265625 * slabs(m1) + nn(twice.astype(BF16), b2[...])
+        root = 1.25 * g - 0.25 * last
         row = lax.broadcasted_iota(jnp.int32, (128, BLOCK), 0)
         row = jnp.where(row < 64, row + starts[0], row + (starts[1] - 64))
         column = lax.broadcasted_iota(jnp.int32, (128, BLOCK), 1)
@@ -282,6 +289,7 @@
 
     @pl.when(core == 1)
     def _():
+        fifth(m1, b2, m2, b3)
         for at in bands:
             g = nn(b0[at], b2[...]) * 0.0625 - 0.3125 * (m0[at] + m1[at])
             t0[at] = g

time: 54.2 us -> 53.9 us (level)
  no operation moved by 1% of the time
where the time goes in v8:
time: 53.9 us; the launch traced here: 53.8 us
  Pallas kernels  53.2 us (99%)
  between operations  0.64 us (1%)
    pallas_call x1, Pallas kernels, on_device(): pl.pallas_call(kernel, out_shape=(pltpu.VMEM((128, 128), BF16), pltpu.VME...  52.1 us

profile of v8, /device:TPU:1, one launch (start us, length us, event | category | flops | bytes accessed | tf_op | source)
XLA Modules:
  0.0 53.8 jit_solution(11656501105429152400)
XLA Ops:
  0.6 52.1 %shard_map.50 = (bf16[128,128]{1,0:T(8,128)(2,1)S(1)}, bf16[8,64,1024]{2,1,0:T(8,128)(2,1)S(1)}) custom-call(bf16[128,4096]{1,0:T(8,128)(2,1)} %a_hbm.1, bf16[4096,128]{1,0:T(8,128)(2,1)} %w_hbm.1, bf16[128,128]{1,0:T(8,128)(2,1)} %b_hbm.1), custom_call_target="tpu_custom_call" | custom-call | tf_op jit(solution)/shard_map/pallas_call | solution.py:378
  52.7 1.0 %shard_map.51 = (bf16[128,128]{1,0:T(8,128)(2,1)}, bf16[8,64,1024]{2,1,0:T(8,128)(2,1)}) custom-call(bf16[128,128]{1,0:T(8,128)(2,1)S(1)} %get-tuple-element.4.out_vmem, bf16[8,64,1024]{2,1,0:T(8,128)(2,1)S(1)} %get-tuple-element.5.upd_vmem), custom_call_target="tpu_custom_call" | custom-call | tf_op jit(solution)/shard_map/pallas_call | solution.py:423

commit v9 on v8

--- a/solution.py
+++ b/solution.py
@@ -264,7 +264,10 @@
     square(m1, b2)
 
     scale = lax.rsqrt(jnp.sqrt(norm))
-    give_half = remote(hbuf, hbuf, ex_send, ex_recv, sibling)
+    def give_half(slab):
+        rows = hbuf.at[pl.ds(slab * 64, 64)]
+        return remote(rows, rows, ex_send.at[slab], ex_recv.at[slab], sibling)
+
 
     @pl.when(core == 0)
     def _():
@@ -283,9 +286,13 @@
         row = jnp.where(row < 64, row + starts[0], row + (starts[1] - 64))
         column = lax.broadcasted_iota(jnp.int32, (128, BLOCK), 1)
         root = (root + jnp.where(row == column, 1.953125, 0.0)) * scale
-        hbuf[...] = nn(root.astype(BF16), u_ref[...]).astype(BF16)
-        give_half.start()
-        give_half.wait_send()
+        root = root.astype(BF16)
+        for slab in (1, 0):
+            at = slice(slab * 64, slab * 64 + 64)
+            hbuf[at] = nn(root[at], u_ref[...]).astype(BF16)
+            give_half(slab).start()
+        for slab in (1, 0):
+            give_half(slab).wait_send()
 
     @pl.when(core == 1)
     def _():
@@ -300,10 +307,6 @@
             t0[:, at] = root
             t0[at, at] = t0[at, at] + jnp.where(eye(HALF), 1.953125, 0.0)
             xr[:, at] = (t0[:, at] * scale).astype(BF16)
-        give_half.wait_recv()
-        piece = (nn(hbuf[...], xr[...]) * math.sqrt(BLOCK)).astype(BF16)
-        osrc[0] = piece[0:64]
-        osrc[1] = piece[64:128]
 
     def place(row_block, cb):
         lanes = pl.ds(pl.multiple_of(cb * BLOCK, BLOCK), BLOCK)
@@ -331,7 +334,13 @@
 
     @pl.when(core == 1)
     def _():
-        for dx, dy in ((1, 2), (1, 6), (0, 2), (0, 6), (1, 1), (1, 7), (0, 1), (0, 7), (1, 0)):
+        for slab in (1, 0):
+            give_half(slab).wait_recv()
+            piece = nn(hbuf[slab * 64 : slab * 64 + 64], xr[...]) * math.sqrt(BLOCK)
+            osrc[slab] = piece.astype(BF16)
+            send_out(slab, 2)
+            send_out(slab, 6)
+        for dx, dy in ((1, 1), (1, 7), (0, 1), (0, 7), (1, 0)):
             send_out(dx, dy)
         remote(osrc.at[0], place(y, c), of_send, of_recv, sibling).start()
         place(y, c)[...] = osrc[0]
@@ -413,7 +422,7 @@
             dma((10,)),
             dma((2, 4)), dma((2, 4)),
             *[dma((2,))] * 12,
-            dma((2, 2)), dma((2, 2)), dma, dma,
+            dma((2, 2)), dma((2, 2)), dma((2,)), dma((2,)),
             dma, dma((2, 8)), dma, dma,
         ],
         compiler_params=pltpu.CompilerParams(

time: 53.9 us -> 53.8 us (level)
  no operation moved by 1% of the time
where the time goes in v9:
time: 53.8 us; the launch traced here: 53.7 us
  Pallas kernels  53 us (99%)
  between operations  0.64 us (1%)
    pallas_call x1, Pallas kernels, on_device(): pl.pallas_call(kernel, out_shape=(pltpu.VMEM((128, 128), BF16), pltpu.VME...  52 us

profile of v9, /device:TPU:1, one launch (start us, length us, event | category | flops | bytes accessed | tf_op | source)
XLA Modules:
  0.0 53.7 jit_solution(13402795748776383961)
XLA Ops:
  0.6 52.0 %shard_map.50 = (bf16[128,128]{1,0:T(8,128)(2,1)S(1)}, bf16[8,64,1024]{2,1,0:T(8,128)(2,1)S(1)}) custom-call(bf16[128,4096]{1,0:T(8,128)(2,1)} %a_hbm.1, bf16[4096,128]{1,0:T(8,128)(2,1)} %w_hbm.1, bf16[128,128]{1,0:T(8,128)(2,1)} %b_hbm.1), custom_call_target="tpu_custom_call" | custom-call | tf_op jit(solution)/shard_map/pallas_call | solution.py:387
  52.6 1.0 %shard_map.51 = (bf16[128,128]{1,0:T(8,128)(2,1)}, bf16[8,64,1024]{2,1,0:T(8,128)(2,1)}) custom-call(bf16[128,128]{1,0:T(8,128)(2,1)S(1)} %get-tuple-element.4.out_vmem, bf16[8,64,1024]{2,1,0:T(8,128)(2,1)S(1)} %get-tuple-element.5.upd_vmem), custom_call_target="tpu_custom_call" | custom-call | tf_op jit(solution)/shard_map/pallas_call | solution.py:432

commit v10 on v8

--- a/solution.py
+++ b/solution.py
@@ -365,7 +365,9 @@
 
 def drain(out_vmem, upd_vmem, out_hbm, upd_hbm, sem):
     copies = [pltpu.make_async_copy(out_vmem, out_hbm, sem.at[8])]
-    copies += [pltpu.make_async_copy(upd_vmem.at[i], upd_hbm.at[i], sem.at[i]) for i in range(8)]
+    for i in range(4):
+        at = pl.ds(2 * i, 2)
+        copies += [pltpu.make_async_copy(upd_vmem.at[at], upd_hbm.at[at], sem.at[i])]
     for copy in copies:
         copy.start()
     for copy in copies:

time: 53.9 us -> 53.9 us (level)
  no operation moved by 1% of the time
where the time goes in v10:
time: 53.9 us; the launch traced here: 53.8 us
  Pallas kernels  53.2 us (99%)
  between operations  0.64 us (1%)
    pallas_call x1, Pallas kernels, on_device(): pl.pallas_call(kernel, out_shape=(pltpu.VMEM((128, 128), BF16), pltpu.VME...  52.1 us

profile of v10, /device:TPU:1, one launch (start us, length us, event | category | flops | bytes accessed | tf_op | source)
XLA Modules:
  0.0 53.8 jit_solution(7422861192648586194)
XLA Ops:
  0.6 52.1 %shard_map.50 = (bf16[128,128]{1,0:T(8,128)(2,1)S(1)}, bf16[8,64,1024]{2,1,0:T(8,128)(2,1)S(1)}) custom-call(bf16[128,4096]{1,0:T(8,128)(2,1)} %a_hbm.1, bf16[4096,128]{1,0:T(8,128)(2,1)} %w_hbm.1, bf16[128,128]{1,0:T(8,128)(2,1)} %b_hbm.1), custom_call_target="tpu_custom_call" | custom-call | tf_op jit(solution)/shard_map/pallas_call | solution.py:380
  52.7 1.1 %shard_map.51 = (bf16[128,128]{1,0:T(8,128)(2,1)}, bf16[8,64,1024]{2,1,0:T(8,128)(2,1)}) custom-call(bf16[128,128]{1,0:T(8,128)(2,1)S(1)} %get-tuple-element.4.out_vmem, bf16[8,64,1024]{2,1,0:T(8,128)(2,1)S(1)} %get-tuple-element.5.upd_vmem), custom_call_target="tpu_custom_call" | custom-call | tf_op jit(solution)/shard_map/pallas_call | solution.py:425
